TPU v7x, 32 devices: a whole 2x2x4 slice. The times are simulated.
32 devices in a mesh: shot: 4 (over y, x), domain: 8 (over z, core).
Axes of the slice: x: 2, y: 2, z: 4, core: 2. Of those that a mesh axis runs over, the one named last changes fastest.
Arguments:
- velsq: float32 [16, 256, 128], P('domain', 'shot'), may hold values from 0.04 to 0.12
- epsilon: float32 [16, 256, 128], P('domain', 'shot'), may hold values from 0 to 0.3
- delta: float32 [16, 256, 128], P('domain', 'shot'), may hold values from 0 to 0.15
- tilt: float32 [16, 256, 128], P('domain', 'shot'), may hold values from -1.2 to 1.2
- azimuth: float32 [16, 256, 128], P('domain', 'shot'), may hold values from -3.140625 to 3.140625
- forward_state: float32 [4, 4, 16, 256, 128], P('shot', None, 'domain'), may hold values from -6 to 6
- adjoint_state: float32 [4, 4, 16, 256, 128], P('shot', None, 'domain'), may hold values from -6 to 6
- wavelet: float32 [4, 2], P('shot'), may hold values from -60 to 60
- source: int32 [4], P('shot'), may hold values from 0 to 524287
- receivers: int32 [4, 256], P('shot'), may hold values from 0 to 524287
- observed: float32 [4, 2, 256], P('shot'), may hold values from -18 to 18
Outputs:
- gradients: float32 [5, 16, 256, 128], P(None, 'domain', 'shot')
Inputs may be any that keep to these rules, and one draw needn't show every extreme that they name: `source`: flat index x * 256 * 128 + y * 128 + z of a grid cell. `receivers`: flat index x * 256 * 128 + y * 128 + z of a grid cell; cells may repeat.
All inputs are finite; a program needn't handle non-finite values.
Results may differ from a plain program's by a relative error of at most 0.0001.
Values sent between devices are 32-bit elements; how exact they have to be, the bound alone decides.
No kernel may reach another device: no remote copies, remote signals or barrier semaphores. Data moves between devices by JAX's collectives and lax.ppermute only.
A program may use at most 128 MiB of HBM per device.

v0:
```python
import functools
import math

import jax
import jax.numpy as jnp
from jax import lax
from jax.experimental import pallas as pl
from jax.experimental.pallas import tpu as pltpu
from jax.sharding import PartitionSpec as P

STEPS = 2
ROWS = 16
PAD = 8
VMEM_LIMIT = 32 * 1024 * 1024
FLOPS_PER_MICRO = 10**9


def half_turn(angle):
    square = angle * angle
    sine = -2.5052108e-08
    for factor in (2.7557319e-06, -1.9841270e-04, 8.3333333e-03, -1.6666667e-01, 1.0):
        sine = sine * square + factor
    cosine = 2.0876757e-09
    for factor in (-2.7557319e-07, 2.4801587e-05, -1.3888889e-03, 4.1666667e-02, -0.5, 1.0):
        cosine = cosine * square + factor
    return sine * angle, cosine


def trig(tilt, azimuth):
    sin_t, cos_t = half_turn(tilt)
    sin_h, cos_h = half_turn(0.5 * azimuth)
    return sin_t, cos_t, 2.0 * sin_h * cos_h, 1.0 - 2.0 * sin_h * sin_h


def even_slab():
    return lax.rem(lax.axis_index("domain"), 2) == 0


def quarter_start(member, quarter):
    return pl.multiple_of((lax.axis_index("shot") ^ member) * quarter, ROWS)


def first_cell(shape):
    return lax.axis_index("domain") * math.prod(shape)


def z_pair(values, lane, edge):
    ahead = pltpu.roll(values, edge, axis=values.ndim - 1)
    behind = pltpu.roll(values, 1, axis=values.ndim - 1)
    return jnp.where(lane == edge, 0.0, ahead), jnp.where(lane == 0, 0.0, behind)


def hessian(padded, field, row, depth, lane, rows=ROWS):
    edge = padded.shape[-1] - 1
    center = padded[field, :, pl.ds(row + PAD, rows), :]
    above = padded[field, :, pl.ds(row + PAD + 1, rows), :]
    below = padded[field, :, pl.ds(row + PAD - 1, rows), :]
    middle = center[1 : 1 + depth]
    double = 2.0 * middle
    curve_xx = center[2:] + center[:depth] - double
    curve_yy = above[1 : 1 + depth] + below[1 : 1 + depth] - double
    ahead, behind = z_pair(middle, lane, edge)
    curve_zz = ahead + behind - double
    slope_x = center[2:] - center[:depth]
    mixed_xy = 0.25 * ((above[2:] - above[:depth]) - (below[2:] - below[:depth]))
    ahead, behind = z_pair(slope_x, lane, edge)
    mixed_xz = 0.25 * (ahead - behind)
    slope_y = above[1 : 1 + depth] - below[1 : 1 + depth]
    ahead, behind = z_pair(slope_y, lane, edge)
    mixed_yz = 0.25 * (ahead - behind)
    return middle, (curve_xx, curve_yy, curve_zz, mixed_xy, mixed_xz, mixed_yz)


def quadratic(weights, hess):
    total = weights[0] * hess[0]
    for weight, part in zip(weights[1:], hess[1:]):
        total = total + weight * part
    return total


def along_of(axis_x, axis_y, axis_z):
    twice_x = 2.0 * axis_x
    return (
        axis_x * axis_x,
        axis_y * axis_y,
        axis_z * axis_z,
        twice_x * axis_y,
        twice_x * axis_z,
        2.0 * axis_y * axis_z,
    )


def flow(hess, axis_x, axis_y, axis_z):
    return (
        hess[0] * axis_x + hess[3] * axis_y + hess[4] * axis_z,
        hess[3] * axis_x + hess[1] * axis_y + hess[5] * axis_z,
        hess[4] * axis_x + hess[5] * axis_y + hess[2] * axis_z,
    )


def cell_kernel(cells):
    depth, width, length = cells.shape

    def chunk(turn, carry):
        row = pl.multiple_of(turn * ROWS, ROWS)
        shape = (depth, ROWS, length)
        plane = lax.broadcasted_iota(jnp.int32, shape, 0)
        line = lax.broadcasted_iota(jnp.int32, shape, 1) + row
        lane = lax.broadcasted_iota(jnp.int32, shape, 2)
        cells[:, pl.ds(row, ROWS), :] = (plane * width + line) * length + lane + first_cell(cells.shape)
        return carry

    lax.fori_loop(0, width // ROWS, chunk, 0)


def pulse_of(source, wave, moment, cells):
    return jnp.where(cells == source[...][None], wave[:, moment : moment + 1][None], 0.0)


def count_kernel(receivers, observed, hits, sums):
    depth, width, length = hits.shape
    count = receivers.shape[1]
    offset = receivers[...] - first_cell(hits.shape)
    inside = (offset >= 0) & (offset < depth * width * length)
    lines = jnp.where(inside, lax.div(offset, length), -1)
    places = lax.rem(offset, length)
    picks = (lax.broadcasted_iota(jnp.int32, (depth * width, count), 0) == lines).astype(jnp.float32)
    lanes = (lax.broadcasted_iota(jnp.int32, (length, count), 0) == places).astype(jnp.float32)
    contract = (((1,), (1,)), ((), ()))
    seen = observed[observed.shape[0] - 1 :, :]
    found = lax.dot_general(picks, lanes, contract, preferred_element_type=jnp.float32)
    total = lax.dot_general(
        picks, lanes * seen, contract, preferred_element_type=jnp.float32, precision=lax.Precision.HIGHEST
    )
    hits[...] = found.reshape(depth, width, length)
    sums[...] = total.reshape(depth, width, length)


def stack_kernel(order, *refs):
    for index, ref in enumerate(refs[:-1]):
        refs[-1][index] = ref[...]


def rim_kernel(order, forward, adjoint, inner, outer):
    depth = forward.shape[1]
    toward = jnp.where(even_slab(), depth - 1, 0)
    for index, (state, member) in enumerate(((forward, 1), (forward, 3), (adjoint, 1), (adjoint, 3))):
        inner[index] = state[member, toward]
        outer[index] = state[member, depth - 1 - toward]


def image_terms(hess_p, hess_q, sin_t, cos_t, sin_a, cos_a):
    axis_x = sin_t * cos_a
    axis_y = sin_t * sin_a
    turn_x = cos_t * cos_a
    turn_y = cos_t * sin_a
    flows = tuple(flow(hess, axis_x, axis_y, cos_t) for hess in (hess_p, hess_q))
    axial_p, axial_q = (axis_x * each[0] + axis_y * each[1] + cos_t * each[2] for each in flows)
    by_tilt = tuple(2.0 * (turn_x * each[0] + turn_y * each[1] - sin_t * each[2]) for each in flows)
    by_spin = tuple(2.0 * (axis_x * each[1] - axis_y * each[0]) for each in flows)
    return (hess_p[0] + hess_p[1] + hess_p[2] - axial_p, axial_q, *by_tilt, *by_spin)


def fill_padded(padded, state, inner, outer, plane):
    depth, width, length = state.shape[1:]
    zeros = jnp.zeros((depth + 2, PAD, length), jnp.float32)
    toward = jnp.where(even_slab(), depth + 1, 0)
    rows = slice(PAD, PAD + width)
    for field, member in enumerate((1, 3)):
        padded[field, :, 0:PAD, :] = zeros
        padded[field, :, PAD + width : 2 * PAD + width, :] = zeros
        padded[field, 1 : 1 + depth, rows, :] = state[member]
        padded[field, toward, rows, :] = inner[plane + field]
        padded[field, depth + 1 - toward, rows, :] = outer[plane + field]


def step(now_p, now_q, old_p, old_q, across, axial, velsq, stretch, root):
    next_p = 2.0 * now_p - old_p + velsq * (stretch * across + root * axial)
    next_q = 2.0 * now_q - old_q + velsq * (root * across + axial)
    return next_p, next_q


def table_of(part, take):
    velsq = part[0, :, take, :]
    stretch = 1.0 + 2.0 * part[1, :, take, :]
    root = jnp.sqrt(1.0 + 2.0 * part[2, :, take, :])
    return (velsq, stretch, root, *trig(part[3, :, take, :], part[4, :, take, :]))


def table_kernel(shots, members, order, *refs):
    parts, table = refs[:-1], refs[-1]
    quarter = table.shape[2] // shots
    for member, part in zip(members, parts):
        start = quarter_start(member, quarter)

        def chunk(turn, carry, part=part, start=start):
            inside = pl.multiple_of(turn * ROWS, ROWS)
            place = pl.ds(pl.multiple_of(start + inside, ROWS), ROWS)
            for index, value in enumerate(table_of(part, pl.ds(inside, ROWS))):
                table[index, :, place, :] = value
            return carry

        lax.fori_loop(0, quarter // ROWS, chunk, 0, unroll=True)


def forward_kernel(shots, members, first, cells, source, wave, forward, *refs):
    refs = list(refs)
    if first:
        parts = {member: None for member in members}
        table, outer, inner, fields, terms, inner_edge, outer_edge, padded = refs
        fill_padded(padded, forward, inner, outer, 0)
    else:
        parts = {member: refs.pop(0) for member in members}
        padded = refs.pop(0)
        table, fields, terms, inner_edge, outer_edge = refs[3:]
    depth, width, length = forward.shape[1:]
    quarter = width // shots
    lane = lax.broadcasted_iota(jnp.int32, (depth, ROWS, length), 2)
    even = even_slab()
    for turn_of, member in enumerate(members):
        start = quarter_start(member, quarter)

        def chunk(turn, carry, part=parts[member], start=start, offset=turn_of * quarter):
            inside = pl.multiple_of(turn * ROWS, ROWS)
            row = pl.multiple_of(start + inside, ROWS)
            place = pl.ds(row, ROWS)
            if part is None:
                values = tuple(table[index, :, place, :] for index in range(7))
            else:
                values = table_of(part, pl.ds(inside, ROWS))
                for index, value in enumerate(values):
                    table[index, :, place, :] = value
            velsq, stretch, root, *turns = values
            now_p, hess_p = hessian(padded, 0, row, depth, lane)
            now_q, hess_q = hessian(padded, 1, row, depth, lane)
            of_image = image_terms(hess_p, hess_q, *turns)
            for index, value in enumerate(of_image):
                terms[index, :, place, :] = value
            next_p, next_q = step(
                now_p, now_q, forward[0, :, place, :], forward[2, :, place, :], *of_image[:2], velsq, stretch, root
            )
            pulse = pulse_of(source, wave, 0, cells[:, place, :])
            side = pl.ds(pl.multiple_of(offset + inside, ROWS), ROWS)
            for index, value in enumerate((next_p + pulse, next_q + pulse)):
                fields[index, :, place, :] = value
                inner_edge[index, side, :] = jnp.where(even, value[depth - 1], value[0])
                outer_edge[index, side, :] = jnp.where(even, value[0], value[depth - 1])
            return carry

        lax.fori_loop(0, quarter // ROWS, chunk, 0, unroll=True)


def backward_kernel(shots, member, first, adjoint, *refs):
    if first:
        inner, outer, table, _, _, late, padded = refs
        fill_padded(padded, adjoint, inner, outer, 2)
    else:
        padded, table, late = refs
    depth, width, length = adjoint.shape[1:]
    quarter = width // shots
    lane = lax.broadcasted_iota(jnp.int32, (depth, ROWS, length), 2)
    start = quarter_start(member, quarter)

    def chunk(turn, carry):
        inside = pl.multiple_of(turn * ROWS, ROWS)
        row = pl.multiple_of(start + inside, ROWS)
        take = pl.ds(inside, ROWS)
        place = pl.ds(row, ROWS)
        velsq, stretch, root, sin_t, cos_t, sin_a, cos_a = (table[index, :, place, :] for index in range(7))
        along = along_of(sin_t * cos_a, sin_t * sin_a, cos_t)
        now_a, hess_a = hessian(padded, 0, row, depth, lane)
        now_b, hess_b = hessian(padded, 1, row, depth, lane)
        across = hess_a[0] + hess_a[1] + hess_a[2] - quadratic(along, hess_a)
        axial = quadratic(along, hess_b)
        late[0, :, take, :], late[1, :, take, :] = step(
            now_a, now_b, adjoint[0, :, place, :], adjoint[2, :, place, :], across, axial, velsq, stretch, root
        )
        return carry

    lax.fori_loop(0, quarter // ROWS, chunk, 0, unroll=True)


def edge_rows(near, rest, shots, quarter, member, row, rows):
    last = shots - 1
    is_near = (member == 0) | (member == last)
    near_row = pl.multiple_of(jnp.where(member == last, quarter, 0) + row, PAD)
    rest_row = pl.multiple_of(jnp.clip(member - 1, 0, last - 2) * quarter + row, PAD)
    return jnp.where(is_near, near[:, pl.ds(near_row, rows), :], rest[:, pl.ds(rest_row, rows), :])


def piece_chunks(quarter, cut):
    pieces = []
    for spans in (((PAD, PAD + cut),), ((0, PAD), (PAD + cut, quarter))):
        chunks = []
        for begin, end in spans:
            chunks += [(row, min(ROWS, end - row)) for row in range(begin, end, ROWS)]
        pieces.append(chunks)
    return pieces


def image_kernel(shots, member, cut, parts, ordered, cells, source, wave, forward, adjoint, fields, outer_near, inner_near,
                 *refs):
    sided = 1 in parts
    refs = list(refs)[1 if ordered else 0 :]
    outer_rest, inner_rest = (refs.pop(0), refs.pop(0)) if sided else (None, None)
    table, terms, late, hits, sums, *refs = refs
    padded = refs.pop()
    came, results = refs[: -len(parts)], refs[-len(parts) :]
    depth, width, length = fields.shape[1:]
    quarter = width // shots
    start = quarter_start(member, quarter)
    toward = jnp.where(even_slab(), depth + 1, 0)
    shot = lax.axis_index("shot")
    spans = (
        (PAD, quarter, start, member, 0, None),
        (0, PAD, jnp.maximum(start - PAD, 0), shot ^ ((shot ^ member) - 1), quarter - PAD, start > 0),
        (PAD + quarter, PAD, jnp.minimum(start + quarter, width - PAD), shot ^ ((shot ^ member) + 1), 0,
         start + quarter < width),
    )
    for target, rows, origin, owner, row, real in spans[: 3 if sided else 1]:
        place = pl.ds(pl.multiple_of(origin, PAD), rows)
        if real is None:
            near = member in (0, shots - 1)
            offset = (quarter if member else 0) if near else (member - 1) * quarter
            outer = (outer_near if near else outer_rest)[:, offset : offset + rows, :]
            inner = (inner_near if near else inner_rest)[:, offset : offset + rows, :]
            center = fields[:, :, place, :]
        else:
            owner = jnp.clip(owner, 0, shots - 1)
            outer = jnp.where(real, edge_rows(outer_near, outer_rest, shots, quarter, owner, row, rows), 0.0)
            inner = jnp.where(real, edge_rows(inner_near, inner_rest, shots, quarter, owner, row, rows), 0.0)
            center = jnp.where(real, fields[:, :, place, :], 0.0)
        padded[:, 1 : 1 + depth, target : target + rows, :] = center
        padded[:, toward, target : target + rows, :] = inner
        padded[:, depth + 1 - toward, target : target + rows, :] = outer
    chunks = [
        (index, inside, rows, sum(size for _, size in piece[:turn]))
        for index, part in enumerate(parts)
        for piece in (piece_chunks(quarter, cut)[part],)
        for turn, (inside, rows) in enumerate(piece)
    ]
    for which, inside, rows, target in chunks:
        lane = lax.broadcasted_iota(jnp.int32, (depth, rows, length), 2)
        place = pl.ds(pl.multiple_of(start + inside, PAD), rows)
        velsq, stretch, root, sin_t, cos_t, sin_a, cos_a = (table[index, :, place, :] for index in range(7))
        axis_x = sin_t * cos_a
        axis_y = sin_t * sin_a
        turn_x = cos_t * cos_a
        turn_y = cos_t * sin_a
        now_p, hess_p = hessian(padded, 0, inside, depth, lane, rows)
        now_q, hess_q = hessian(padded, 1, inside, depth, lane, rows)
        along = along_of(axis_x, axis_y, cos_t)
        across = hess_p[0] + hess_p[1] + hess_p[2] - quadratic(along, hess_p)
        axial = quadratic(along, hess_q)
        drive_p = stretch * across + root * axial
        drive_q = root * across + axial
        pulse = pulse_of(source, wave, 1, cells[:, place, :])
        next_p = 2.0 * now_p - forward[1, :, place, :] + velsq * drive_p + pulse
        late_a = adjoint[1, :, place, :]
        late_b = adjoint[3, :, place, :]
        early_a = late[0, :, inside : inside + rows, :] + (hits[:, place, :] * next_p - sums[:, place, :])
        early_b = late[1, :, inside : inside + rows, :]
        push_q = root * late_a + late_b
        push_p = stretch * late_a + root * late_b
        mixed = tuple(push_q * of_q - push_p * of_p for of_q, of_p in zip(hess_q, hess_p))
        pull = flow(mixed, axis_x, axis_y, cos_t)
        tilt_sum = 2.0 * (turn_x * pull[0] + turn_y * pull[1] - sin_t * pull[2])
        spin_sum = 2.0 * (axis_x * pull[1] - axis_y * pull[0])
        across_0, axial_0, tilt_p, tilt_q, spin_p, spin_q = (terms[index, :, place, :] for index in range(6))
        push_q = root * early_a + early_b
        push_p = stretch * early_a + root * early_b
        tilt_sum = tilt_sum + push_q * tilt_q - push_p * tilt_p
        spin_sum = spin_sum + push_q * spin_q - push_p * spin_p
        images = (
            late_a * drive_p + late_b * drive_q + push_p * across_0 + push_q * axial_0,
            2.0 * velsq * (late_a * across + early_a * across_0),
            velsq * (late_a * axial + late_b * across + early_a * axial_0 + early_b * across_0) / root,
            velsq * tilt_sum,
            velsq * spin_sum,
        )
        target = slice(target, target + rows)
        for index, image in enumerate(images):
            results[which][index, :, target, :] = image + came[which][index, :, target, :] if came else image


def add_kernel(one, more, order, total):
    total[...] = one[...] + more[...]


def total_kernel(count, cut, *refs):
    total = refs[-1]
    for group, chunks in zip((refs[:count], refs[count : 2 * count]), piece_chunks(total.shape[2], cut)):
        source = 0
        for row, rows in chunks:
            sum_of = group[0][:, :, source : source + rows, :]
            for ref in group[1:]:
                sum_of = sum_of + ref[:, :, source : source + rows, :]
            total[:, :, row : row + rows, :] = sum_of
            source += rows


VMEM = pl.BlockSpec(memory_space=pltpu.VMEM)


def call(kernel, outs, micros, *operands, scratch=(), out_space=VMEM, aliases=None):
    moved = sum(4 * operand.size for operand in operands) + sum(4 * out.size for out in outs)
    return pl.pallas_call(
        kernel,
        out_shape=outs,
        in_specs=[VMEM] * len(operands),
        out_specs=[out_space] * len(outs),
        scratch_shapes=list(scratch),
        input_output_aliases=aliases or {},
        compiler_params=pltpu.CompilerParams(vmem_limit_bytes=VMEM_LIMIT),
        cost_estimate=pl.CostEstimate(flops=int(micros * FLOPS_PER_MICRO), bytes_accessed=moved, transcendentals=0),
    )(*operands)


def floats(*shape):
    return jax.ShapeDtypeStruct(shape, jnp.float32)


def shards(
    velsq,
    epsilon,
    delta,
    tilt,
    azimuth,
    forward_state,
    adjoint_state,
    wavelet,
    source,
    receivers,
    observed,
):
    shots = lax.axis_size("shot")
    slabs = lax.axis_size("domain")
    depth, quarter, length = velsq.shape
    width = quarter * shots
    tree = shots == 4

    def swap(values, member):
        return lax.ppermute(values, "shot", [(index, index ^ member) for index in range(shots)])

    def pair(values, first):
        pairs = [(index, index + 1) for index in range(first, slabs - 1, 2)]
        return lax.ppermute(values, "domain", pairs + [(target, source) for source, target in pairs])

    before = forward_state[0]
    after = adjoint_state[0]
    wave = wavelet
    spot = source[None, :]
    slab_shape = floats(depth, width, length)
    cut = max(5 * quarter // 8 // PAD * PAD, PAD)
    piece_shapes = [floats(5, depth, cut, length), floats(5, depth, quarter - cut, length)]
    edges = floats(2, width, length)
    coefficients = (velsq, epsilon, delta, tilt, azimuth)
    cells = call(cell_kernel, [jax.ShapeDtypeStruct((depth, width, length), jnp.int32)], 1.5)[0]
    (own,) = call(stack_kernel, [floats(5, depth, quarter, length)], 0.3, cells, *coefficients)
    rims = floats(4, width, length)
    inner, outer = call(rim_kernel, [rims, rims], 0.4, own, before, after)
    hits, sums = call(count_kernel, [slab_shape, slab_shape], 1.5, receivers, observed[0])
    parts = [swap(own, member) if member else own for member in range(shots)]
    outer = pair(outer, 1)
    inner = pair(inner, 0)
    two = floats(2, depth, width, length)
    wide = floats(7, depth, width, length)
    ringed = (2, depth + 2, width + 2 * PAD, length)
    last = shots - 1
    (table,) = call(functools.partial(table_kernel, shots, (0, last)), [wide], 3.0, hits, own, parts[last])
    near = floats(2, 2 * quarter, length)
    six = floats(6, depth, width, length)
    fields, terms, inner_near, outer_near, early = call(
        functools.partial(forward_kernel, shots, (0, last), True),
        [two, six, near, near, floats(*ringed)],
        1.2,
        cells, spot, wave, before, table, outer, inner,
    )
    outer_near = pair(outer_near, 1)
    inner_near = pair(inner_near, 0)
    middle = range(1, last)
    rest = floats(2, len(middle) * quarter, length)
    table, fields, terms, inner_rest, outer_rest = call(
        functools.partial(forward_kernel, shots, middle, False),
        [wide, two, six, rest, rest],
        0.6 * len(middle),
        cells, spot, wave, before, *(parts[member] for member in middle), early, table, fields, terms,
        aliases={5 + len(middle) + index: index for index in range(3)},
    )
    outer_rest = pair(outer_rest, 1)
    inner_rest = pair(inner_rest, 0)
    late_shape = floats(2, depth, quarter, length)
    late_last, ring = call(
        functools.partial(backward_kernel, shots, last, True), [late_shape, floats(*ringed)], 0.8,
        after, inner, outer, table, outer_near, inner_near,
    )

    def late_of(member):
        if member == last:
            return late_last
        return call(
            functools.partial(backward_kernel, shots, member, False), [late_shape], 0.6, after, ring, table
        )[0]

    def image(member, parts=(0, 1), came=(), order=()):
        rest_edges = (outer_rest, inner_rest) if 1 in parts else ()
        return call(
            functools.partial(image_kernel, shots, member, cut, parts, bool(order)), [piece_shapes[part] for part in parts], 1.2,
            cells, spot, wave, before, after, fields, outer_near, inner_near, *order, *rest_edges,
            table, terms, late_of(member), hits, sums, *came,
            scratch=[pltpu.VMEM((2, depth + 2, quarter + 2 * PAD, length), jnp.float32)],
        )

    if tree:
        (far_first,) = image(3, (0,))
        from_x = swap(far_first, 1)
        (far_second,) = image(3, (1,), order=(far_first,))
        from_y = swap(far_second, 2)
        y_first, y_second = image(2, order=(far_second,))
        near_y = swap(y_second, 2)
        x_first, x_second = image(1, order=(y_second,))
        near_x = swap(x_first, 1)
        (y_first,) = call(add_kernel, piece_shapes[:1], 0.1, y_first, from_x, far_first)
        over_y = swap(y_first, 2)
        (x_second,) = call(add_kernel, piece_shapes[1:], 0.1, x_second, from_y, y_first)
        over_x = swap(x_second, 1)
        (own_second,) = image(0, (1,), came=(near_y,))
        (own_first,) = image(0, (0,), came=(near_x,), order=(own_second,))
        groups = [own_first, over_y, own_second, over_x]
    else:
        sums_of = {member: image(member) for member in reversed(range(shots))}
        groups = [swap(sums_of[member][part], member) if member else sums_of[0][part]
                  for part in range(2) for member in range(shots)]
    return call(
        functools.partial(total_kernel, len(groups) // 2, cut),
        [floats(5, depth, quarter, length)], 0.8, *groups, out_space=pl.BlockSpec(),
    )[0]


def solution(mesh):
    placed = (
        P("domain", "shot", None),
        P("domain", "shot", None),
        P("domain", "shot", None),
        P("domain", "shot", None),
        P("domain", "shot", None),
        P("shot", None, "domain", None, None),
        P("shot", None, "domain", None, None),
        P("shot", None),
        P("shot"),
        P("shot", None),
        P("shot", None, None),
    )
    return jax.shard_map(
        shards,
        mesh=mesh,
        in_specs=placed,
        out_specs=P(None, "domain", "shot", None),
        check_vma=False,
    )
```

profile of v0, /device:TPU:0, one launch (start us, length us, event | category | flops | bytes accessed | tf_op | source)
XLA Modules:
  0.0 40.7 jit_solution(3921774287603959703)
XLA Ops:
  0.2 0.6 %copy-done.7 = f32[2,64,128]{2,1,0:T(8,128)S(1)} copy-done((f32[2,64,128]{2,1,0:T(8,128)S(1)}, f32[2,64,128]{2,1,0:T(8,128)}, u32[]{:S(2)}) %copy-start.7) | copy-done | bytes 65560
  1.0 4.0 %collective-permute-start.2 = (f32[5,2,64,128]{3,2,1,0:T(8,128)S(1)}, f32[5,2,64,128]{3,2,1,0:T(8,128)S(1)}, u32[]{:S(2)}, u32[]{:S(2)}) collective-permute-start(f32[5,2,64,128]{3,2,1,0:T(8,128)S(1)} %shard_map.110.refs_0_.order), channel_id=1, source_target_pairs={{0,24},{8,16},{16,8},{24,0},{1,25},{9,17},{17,9},{25,1},{2,26},{10... | collective-permute-start | bytes 983048 | tf_op jit(solution)/shard_map/ppermute | solution.py:443
  5.0 0.7 %collective-permute-start.3 = (f32[4,256,128]{2,1,0:T(8,128)S(1)}, f32[4,256,128]{2,1,0:T(8,128)S(1)}, u32[]{:S(2)}, u32[]{:S(2)}) collective-permute-start(f32[4,256,128]{2,1,0:T(8,128)S(1)} %get-tuple-element.26), channel_id=1, source_target_pairs={{1,2},{3,4},{5,6},{2,1},{4,3},{6,5},{9,10},{11,12},{13,14},{10,9},... | collective-permute-start | bytes 1572872 | tf_op jit(solution)/shard_map/ppermute | solution.py:447
  5.7 3.0 %collective-permute-start.4 = (f32[4,256,128]{2,1,0:T(8,128)S(1)}, f32[4,256,128]{2,1,0:T(8,128)S(1)}, u32[]{:S(2)}, u32[]{:S(2)}) collective-permute-start(f32[4,256,128]{2,1,0:T(8,128)S(1)} %get-tuple-element.27), channel_id=1, source_target_pairs={{0,1},{2,3},{4,5},{6,7},{1,0},{3,2},{5,4},{7,6},{8,9},{10,11},{12,... | collective-permute-start | bytes 1572872 | tf_op jit(solution)/shard_map/ppermute | solution.py:447
  9.2 1.3 %collective-permute-start = (f32[5,2,64,128]{3,2,1,0:T(8,128)S(1)}, f32[5,2,64,128]{3,2,1,0:T(8,128)S(1)}, u32[]{:S(2)}, u32[]{:S(2)}) collective-permute-start(f32[5,2,64,128]{3,2,1,0:T(8,128)S(1)} %shard_map.110.refs_0_.order), channel_id=1, source_target_pairs={{0,8},{8,0},{16,24},{24,16},{1,9},{9,1},{17,25},{25,17},{2,10},{10... | collective-permute-start | bytes 983048 | tf_op jit(solution)/shard_map/ppermute | solution.py:443
  11.1 0.7 %shard_map.111 = (f32[2,256,128]{2,1,0:T(8,128)S(1)}, f32[2,256,128]{2,1,0:T(8,128)S(1)}) custom-call(s32[1,256]{1,0:T(1,128)S(1)} %copy-done.9, f32[2,256]{1,0:T(2,128)S(1)} %bitcast.32), custom_call_target="tpu_custom_call" | custom-call | flops 1500000000 | bytes 527360 | tf_op jit(solution)/shard_map/pallas_call | solution.py:407
  11.8 1.3 %collective-permute-done.2.refs_1_ = f32[5,2,64,128]{3,2,1,0:T(8,128)S(1)} collective-permute-done((f32[5,2,64,128]{3,2,1,0:T(8,128)S(1)}, f32[5,2,64,128]{3,2,1,0:T(8,128)S(1)}, u32[]{:S(2)}, u32[]{:S(2)}) %collective-permute-start.2) | collective-permute-done | bytes 327712 | tf_op jit(solution)/shard_map/ppermute | solution.py:443
  13.7 0.8 %shard_map.114 = (f32[2,2,256,128]{3,2,1,0:T(8,128)S(1)}, f32[6,2,256,128]{3,2,1,0:T(8,128)S(1)}, f32[2,128,128]{2,1,0:T(8,128)S(1)}, f32[2,128,128]{2,1,0:T(8,128)S(1)}, f32[2,4,272,128]{3,2,1,0:T(8,128)S(1)}) custom-call(s32[2,256,128]{2,1,0:T(8,128)S(1)} %shard_map.109.order.cells, s32[1,1]{1,0:T(1,128)} %bitcast.4.source, f32[1,2]{1,0:T(1,128)S(1)} %copy-done.2, ...), custom_call_target="tpu_custom_call" | custom-call | flops 1200000000 | bytes 7667724 | tf_op jit(solution)/shard_map/pallas_call | solution.py:407
  14.6 0.7 %collective-permute-start.5 = (f32[2,128,128]{2,1,0:T(8,128)S(1)}, f32[2,128,128]{2,1,0:T(8,128)S(1)}, u32[]{:S(2)}, u32[]{:S(2)}) collective-permute-start(f32[2,128,128]{2,1,0:T(8,128)S(1)} %get-tuple-element.32), channel_id=1, source_target_pairs={{1,2},{3,4},{5,6},{2,1},{4,3},{6,5},{9,10},{11,12},{13,14},{10,9},... | collective-permute-start | bytes 393224 | tf_op jit(solution)/shard_map/ppermute | solution.py:447
  15.3 4.8 %collective-permute-start.6 = (f32[2,128,128]{2,1,0:T(8,128)S(1)}, f32[2,128,128]{2,1,0:T(8,128)S(1)}, u32[]{:S(2)}, u32[]{:S(2)}) collective-permute-start(f32[2,128,128]{2,1,0:T(8,128)S(1)} %get-tuple-element.33), channel_id=1, source_target_pairs={{0,1},{2,3},{4,5},{6,7},{1,0},{3,2},{5,4},{7,6},{8,9},{10,11},{12,... | collective-permute-start | bytes 393224 | tf_op jit(solution)/shard_map/ppermute | solution.py:447
  20.1 0.9 %shard_map.115 = (f32[7,2,256,128]{3,2,1,0:T(8,128)S(1)}, f32[2,2,256,128]{3,2,1,0:T(8,128)S(1)}, f32[6,2,256,128]{3,2,1,0:T(8,128)S(1)}, f32[2,128,128]{2,1,0:T(8,128)S(1)}, f32[2,128,128]{2,1,0:T(8,128)S(1)}) custom-call(s32[2,256,128]{2,1,0:T(8,128)S(1)} %shard_map.109.order.cells, ...), custom_call_target="tpu_custom_call", output_to_operand_aliasing={{0}: (7, {}), {1}: (8, {}), {2}: (9, {})} | custom-call | flops 1200000000 | bytes 11206668 | tf_op jit(solution)/shard_map/pallas_call | solution.py:407
  21.0 0.7 %collective-permute-start.7 = (f32[2,128,128]{2,1,0:T(8,128)S(1)}, f32[2,128,128]{2,1,0:T(8,128)S(1)}, u32[]{:S(2)}, u32[]{:S(2)}) collective-permute-start(f32[2,128,128]{2,1,0:T(8,128)S(1)} %get-tuple-element.34), channel_id=1, source_target_pairs={{1,2},{3,4},{5,6},{2,1},{4,3},{6,5},{9,10},{11,12},{13,14},{10,9},... | collective-permute-start | bytes 393224 | tf_op jit(solution)/shard_map/ppermute | solution.py:447
  21.7 3.0 %collective-permute-start.8 = (f32[2,128,128]{2,1,0:T(8,128)S(1)}, f32[2,128,128]{2,1,0:T(8,128)S(1)}, u32[]{:S(2)}, u32[]{:S(2)}) collective-permute-start(f32[2,128,128]{2,1,0:T(8,128)S(1)} %get-tuple-element.35), channel_id=1, source_target_pairs={{0,1},{2,3},{4,5},{6,7},{1,0},{3,2},{5,4},{7,6},{8,9},{10,11},{12,... | collective-permute-start | bytes 393224 | tf_op jit(solution)/shard_map/ppermute | solution.py:447
  25.5 1.4 %collective-permute-start.11 = (f32[5,2,40,128]{3,2,1,0:T(8,128)S(1)}, f32[5,2,40,128]{3,2,1,0:T(8,128)S(1)}, u32[]{:S(2)}, u32[]{:S(2)}) collective-permute-start(f32[5,2,40,128]{3,2,1,0:T(8,128)S(1)} %shard_map.118.refs_0_.order), channel_id=1, source_target_pairs={{0,8},{8,0},{16,24},{24,16},{1,9},{9,1},{17,25},{25,17},{2,10},{10... | collective-permute-start | bytes 614408 | tf_op jit(solution)/shard_map/ppermute | solution.py:443
  27.9 1.5 %collective-permute-start.13 = (f32[5,2,24,128]{3,2,1,0:T(8,128)S(1)}, f32[5,2,24,128]{3,2,1,0:T(8,128)S(1)}, u32[]{:S(2)}, u32[]{:S(2)}) collective-permute-start(f32[5,2,24,128]{3,2,1,0:T(8,128)S(1)} %shard_map.119.refs_0_), channel_id=1, source_target_pairs={{0,16},{8,24},{16,0},{24,8},{1,17},{9,25},{17,1},{25,9},{2,18},{10... | collective-permute-start | bytes 368648 | tf_op jit(solution)/shard_map/ppermute | solution.py:443
  29.4 0.5 %shard_map.121 = (f32[5,2,40,128]{3,2,1,0:T(8,128)S(1)}, f32[5,2,24,128]{3,2,1,0:T(8,128)S(1)}) custom-call(s32[2,256,128]{2,1,0:T(8,128)S(1)} %shard_map.109.order.cells, s32[1,1]{1,0:T(1,128)} %bitcast.8.source, f32[1,2]{1,0:T(1,128)S(1)} %copy-done.2, f32[4,2,256,128]{3,2,1,0:T(8,128)S(1)} %bitcast.28, f32[4,2,256,128]{3,2,1,0:T(8,128)S(1)} %bitcast.18, ...), custom_call_target="tpu_custom_call" | custom-call | flops 1200000000 | bytes 7921676 | tf_op jit(solution)/shard_map/pallas_call | solution.py:407
  29.9 0.6 %collective-permute-start.9 = (f32[5,2,24,128]{3,2,1,0:T(8,128)S(1)}, f32[5,2,24,128]{3,2,1,0:T(8,128)S(1)}, u32[]{:S(2)}, u32[]{:S(2)}) collective-permute-start(f32[5,2,24,128]{3,2,1,0:T(8,128)S(1)} %get-tuple-element.41.refs_0_), channel_id=1, source_target_pairs={{0,16},{8,24},{16,0},{24,8},{1,17},{9,25},{17,1},{25,9},{2,18},{10... | collective-permute-start | bytes 368648 | tf_op jit(solution)/shard_map/ppermute | solution.py:443
  31.1 0.7 %collective-permute-start.10 = (f32[5,2,40,128]{3,2,1,0:T(8,128)S(1)}, f32[5,2,40,128]{3,2,1,0:T(8,128)S(1)}, u32[]{:S(2)}, u32[]{:S(2)}) collective-permute-start(f32[5,2,40,128]{3,2,1,0:T(8,128)S(1)} %get-tuple-element.42), channel_id=1, source_target_pairs={{0,8},{8,0},{16,24},{24,16},{1,9},{9,1},{17,25},{25,17},{2,10},{10... | collective-permute-start | bytes 614408 | tf_op jit(solution)/shard_map/ppermute | solution.py:443
  32.6 1.4 %collective-permute-start.12 = (f32[5,2,40,128]{3,2,1,0:T(8,128)S(1)}, f32[5,2,40,128]{3,2,1,0:T(8,128)S(1)}, u32[]{:S(2)}, u32[]{:S(2)}) collective-permute-start(f32[5,2,40,128]{3,2,1,0:T(8,128)S(1)} %shard_map.126.order), channel_id=1, source_target_pairs={{0,16},{8,24},{16,0},{24,8},{1,17},{9,25},{17,1},{25,9},{2,18},{10... | collective-permute-start | bytes 614408 | tf_op jit(solution)/shard_map/ppermute | solution.py:443
  34.0 1.6 %collective-permute-start.14 = (f32[5,2,24,128]{3,2,1,0:T(8,128)S(1)}, f32[5,2,24,128]{3,2,1,0:T(8,128)S(1)}, u32[]{:S(2)}, u32[]{:S(2)}) collective-permute-start(f32[5,2,24,128]{3,2,1,0:T(8,128)S(1)} %shard_map.127), channel_id=1, source_target_pairs={{0,8},{8,0},{16,24},{24,16},{1,9},{9,1},{17,25},{25,17},{2,10},{10... | collective-permute-start | bytes 368648 | tf_op jit(solution)/shard_map/ppermute | solution.py:443
  35.5 0.9 %collective-permute-done.9.refs_7_ = f32[5,2,24,128]{3,2,1,0:T(8,128)S(1)} collective-permute-done((f32[5,2,24,128]{3,2,1,0:T(8,128)S(1)}, f32[5,2,24,128]{3,2,1,0:T(8,128)S(1)}, u32[]{:S(2)}, u32[]{:S(2)}) %collective-permute-start.9) | collective-permute-done | bytes 122912 | tf_op jit(solution)/shard_map/ppermute | solution.py:443
  36.7 2.0 %collective-permute-done.10.refs_6_ = f32[5,2,40,128]{3,2,1,0:T(8,128)S(1)} collective-permute-done((f32[5,2,40,128]{3,2,1,0:T(8,128)S(1)}, f32[5,2,40,128]{3,2,1,0:T(8,128)S(1)}, u32[]{:S(2)}, u32[]{:S(2)}) %collective-permute-start.10) | collective-permute-done | bytes 204832 | tf_op jit(solution)/shard_map/ppermute | solution.py:443
  39.0 0.9 %collective-permute-done.14.refs_3_ = f32[5,2,24,128]{3,2,1,0:T(8,128)S(1)} collective-permute-done((f32[5,2,24,128]{3,2,1,0:T(8,128)S(1)}, f32[5,2,24,128]{3,2,1,0:T(8,128)S(1)}, u32[]{:S(2)}, u32[]{:S(2)}) %collective-permute-start.14) | collective-permute-done | bytes 122912 | tf_op jit(solution)/shard_map/ppermute | solution.py:443
  40.0 0.8 %shard_map.128 = f32[5,2,64,128]{3,2,1,0:T(8,128)} custom-call(f32[5,2,40,128]{3,2,1,0:T(8,128)S(1)} %shard_map.125.refs_0_, f32[5,2,40,128]{3,2,1,0:T(8,128)S(1)} %collective-permute-done.12.refs_1_, f32[5,2,24,128]{3,2,1,0:T(8,128)S(1)} %shard_map.122.refs_0_.refs_2_, f32[5,2,24,128]{3,2,1,0:T(8,128)S(1)} %collective-permute-done.14.refs_3_), custom_call_target="tpu_custom_call" | custom-call | flops 800000000 | bytes 983040 | tf_op jit(solution)/shard_map/pallas_call | solution.py:407
  (46 shorter events, 5.1 us)
Async XLA Ops:
  0.0 0.8 %copy-start.7 = (f32[2,64,128]{2,1,0:T(8,128)S(1)}, f32[2,64,128]{2,1,0:T(8,128)}, u32[]{:S(2)}) copy-start(f32[2,64,128]{2,1,0:T(8,128)} %refs_4_.1) | copy-start | bytes 196612
  0.0 0.9 %copy-start.6 = (f32[2,64,128]{2,1,0:T(8,128)S(1)}, f32[2,64,128]{2,1,0:T(8,128)}, u32[]{:S(2)}) copy-start(f32[2,64,128]{2,1,0:T(8,128)} %refs_3_.1) | copy-start | bytes 196612
  0.0 0.9 %copy-start.5 = (f32[2,64,128]{2,1,0:T(8,128)S(1)}, f32[2,64,128]{2,1,0:T(8,128)}, u32[]{:S(2)}) copy-start(f32[2,64,128]{2,1,0:T(8,128)} %refs_2_.1) | copy-start | bytes 196612
  0.0 0.9 %copy-start.4 = (f32[2,64,128]{2,1,0:T(8,128)S(1)}, f32[2,64,128]{2,1,0:T(8,128)}, u32[]{:S(2)}) copy-start(f32[2,64,128]{2,1,0:T(8,128)} %refs_1_.1) | copy-start | bytes 196612
  0.0 1.0 %copy-start.3 = (f32[2,64,128]{2,1,0:T(8,128)S(1)}, f32[2,64,128]{2,1,0:T(8,128)}, u32[]{:S(2)}) copy-start(f32[2,64,128]{2,1,0:T(8,128)} %refs_0_.1) | copy-start | bytes 196612
  0.0 4.9 %copy-start.1 = (f32[1,4,2,256,128]{4,3,2,1,0:T(8,128)S(1)}, f32[1,4,2,256,128]{4,3,2,1,0:T(8,128)}, u32[]{:S(2)}) copy-start(f32[1,4,2,256,128]{4,3,2,1,0:T(8,128)} %param.16) | copy-start | bytes 3145732
  1.0 4.0 %copy-start = (f32[1,4,2,256,128]{4,3,2,1,0:T(8,128)S(1)}, f32[1,4,2,256,128]{4,3,2,1,0:T(8,128)}, u32[]{:S(2)}) copy-start(f32[1,4,2,256,128]{4,3,2,1,0:T(8,128)} %param.17) | copy-start | bytes 3145732
  1.0 10.2 %copy-start.8 = (f32[1,2,256]{2,1,0:T(2,128)S(1)}, f32[1,2,256]{2,1,0:T(2,128)}, u32[]{:S(2)}) copy-start(f32[1,2,256]{2,1,0:T(2,128)} %param.21) | copy-start | bytes 6148
  1.0 10.2 %copy-start.9 = (s32[1,256]{1,0:T(1,128)S(1)}, s32[1,256]{1,0:T(1,128)}, u32[]{:S(2)}) copy-start(s32[1,256]{1,0:T(1,128)} %receivers.1) | copy-start | bytes 3076
  1.0 12.1 %collective-permute-start.2 = (f32[5,2,64,128]{3,2,1,0:T(8,128)S(1)}, f32[5,2,64,128]{3,2,1,0:T(8,128)S(1)}, u32[]{:S(2)}, u32[]{:S(2)}) collective-permute-start(f32[5,2,64,128]{3,2,1,0:T(8,128)S(1)} %shard_map.110.refs_0_.order), channel_id=1, source_target_pairs={{0,24},{8,16},{16,8},{24,0},{1,25},{9,17},{17,9},{25,1},{2,26},{10... | collective-permute-start | bytes 983048 | tf_op jit(solution)/shard_map/ppermute | solution.py:443
  5.0 8.3 %collective-permute-start.3 = (f32[4,256,128]{2,1,0:T(8,128)S(1)}, f32[4,256,128]{2,1,0:T(8,128)S(1)}, u32[]{:S(2)}, u32[]{:S(2)}) collective-permute-start(f32[4,256,128]{2,1,0:T(8,128)S(1)} %get-tuple-element.26), channel_id=1, source_target_pairs={{1,2},{3,4},{5,6},{2,1},{4,3},{6,5},{9,10},{11,12},{13,14},{10,9},... | collective-permute-start | bytes 1572872 | tf_op jit(solution)/shard_map/ppermute | solution.py:447
  5.7 7.7 %collective-permute-start.4 = (f32[4,256,128]{2,1,0:T(8,128)S(1)}, f32[4,256,128]{2,1,0:T(8,128)S(1)}, u32[]{:S(2)}, u32[]{:S(2)}) collective-permute-start(f32[4,256,128]{2,1,0:T(8,128)S(1)} %get-tuple-element.27), channel_id=1, source_target_pairs={{0,1},{2,3},{4,5},{6,7},{1,0},{3,2},{5,4},{7,6},{8,9},{10,11},{12,... | collective-permute-start | bytes 1572872 | tf_op jit(solution)/shard_map/ppermute | solution.py:447
  8.7 11.4 %collective-permute-start.1 = (f32[5,2,64,128]{3,2,1,0:T(8,128)S(1)}, f32[5,2,64,128]{3,2,1,0:T(8,128)S(1)}, u32[]{:S(2)}, u32[]{:S(2)}) collective-permute-start(f32[5,2,64,128]{3,2,1,0:T(8,128)S(1)} %shard_map.110.refs_0_.order), channel_id=1, source_target_pairs={{0,16},{8,24},{16,0},{24,8},{1,17},{9,25},{17,1},{25,9},{2,18},{10... | collective-permute-start | bytes 983048 | tf_op jit(solution)/shard_map/ppermute | solution.py:443
  9.2 10.9 %collective-permute-start = (f32[5,2,64,128]{3,2,1,0:T(8,128)S(1)}, f32[5,2,64,128]{3,2,1,0:T(8,128)S(1)}, u32[]{:S(2)}, u32[]{:S(2)}) collective-permute-start(f32[5,2,64,128]{3,2,1,0:T(8,128)S(1)} %shard_map.110.refs_0_.order), channel_id=1, source_target_pairs={{0,8},{8,0},{16,24},{24,16},{1,9},{9,1},{17,25},{25,17},{2,10},{10... | collective-permute-start | bytes 983048 | tf_op jit(solution)/shard_map/ppermute | solution.py:443
  14.6 10.1 %collective-permute-start.5 = (f32[2,128,128]{2,1,0:T(8,128)S(1)}, f32[2,128,128]{2,1,0:T(8,128)S(1)}, u32[]{:S(2)}, u32[]{:S(2)}) collective-permute-start(f32[2,128,128]{2,1,0:T(8,128)S(1)} %get-tuple-element.32), channel_id=1, source_target_pairs={{1,2},{3,4},{5,6},{2,1},{4,3},{6,5},{9,10},{11,12},{13,14},{10,9},... | collective-permute-start | bytes 393224 | tf_op jit(solution)/shard_map/ppermute | solution.py:447
  15.3 9.4 %collective-permute-start.6 = (f32[2,128,128]{2,1,0:T(8,128)S(1)}, f32[2,128,128]{2,1,0:T(8,128)S(1)}, u32[]{:S(2)}, u32[]{:S(2)}) collective-permute-start(f32[2,128,128]{2,1,0:T(8,128)S(1)} %get-tuple-element.33), channel_id=1, source_target_pairs={{0,1},{2,3},{4,5},{6,7},{1,0},{3,2},{5,4},{7,6},{8,9},{10,11},{12,... | collective-permute-start | bytes 393224 | tf_op jit(solution)/shard_map/ppermute | solution.py:447
  21.0 6.5 %collective-permute-start.7 = (f32[2,128,128]{2,1,0:T(8,128)S(1)}, f32[2,128,128]{2,1,0:T(8,128)S(1)}, u32[]{:S(2)}, u32[]{:S(2)}) collective-permute-start(f32[2,128,128]{2,1,0:T(8,128)S(1)} %get-tuple-element.34), channel_id=1, source_target_pairs={{1,2},{3,4},{5,6},{2,1},{4,3},{6,5},{9,10},{11,12},{13,14},{10,9},... | collective-permute-start | bytes 393224 | tf_op jit(solution)/shard_map/ppermute | solution.py:447
  21.7 5.9 %collective-permute-start.8 = (f32[2,128,128]{2,1,0:T(8,128)S(1)}, f32[2,128,128]{2,1,0:T(8,128)S(1)}, u32[]{:S(2)}, u32[]{:S(2)}) collective-permute-start(f32[2,128,128]{2,1,0:T(8,128)S(1)} %get-tuple-element.35), channel_id=1, source_target_pairs={{0,1},{2,3},{4,5},{6,7},{1,0},{3,2},{5,4},{7,6},{8,9},{10,11},{12,... | collective-permute-start | bytes 393224 | tf_op jit(solution)/shard_map/ppermute | solution.py:447
  25.5 7.1 %collective-permute-start.11 = (f32[5,2,40,128]{3,2,1,0:T(8,128)S(1)}, f32[5,2,40,128]{3,2,1,0:T(8,128)S(1)}, u32[]{:S(2)}, u32[]{:S(2)}) collective-permute-start(f32[5,2,40,128]{3,2,1,0:T(8,128)S(1)} %shard_map.118.refs_0_.order), channel_id=1, source_target_pairs={{0,8},{8,0},{16,24},{24,16},{1,9},{9,1},{17,25},{25,17},{2,10},{10... | collective-permute-start | bytes 614408 | tf_op jit(solution)/shard_map/ppermute | solution.py:443
  27.9 6.1 %collective-permute-start.13 = (f32[5,2,24,128]{3,2,1,0:T(8,128)S(1)}, f32[5,2,24,128]{3,2,1,0:T(8,128)S(1)}, u32[]{:S(2)}, u32[]{:S(2)}) collective-permute-start(f32[5,2,24,128]{3,2,1,0:T(8,128)S(1)} %shard_map.119.refs_0_), channel_id=1, source_target_pairs={{0,16},{8,24},{16,0},{24,8},{1,17},{9,25},{17,1},{25,9},{2,18},{10... | collective-permute-start | bytes 368648 | tf_op jit(solution)/shard_map/ppermute | solution.py:443
  29.9 6.5 %collective-permute-start.9 = (f32[5,2,24,128]{3,2,1,0:T(8,128)S(1)}, f32[5,2,24,128]{3,2,1,0:T(8,128)S(1)}, u32[]{:S(2)}, u32[]{:S(2)}) collective-permute-start(f32[5,2,24,128]{3,2,1,0:T(8,128)S(1)} %get-tuple-element.41.refs_0_), channel_id=1, source_target_pairs={{0,16},{8,24},{16,0},{24,8},{1,17},{9,25},{17,1},{25,9},{2,18},{10... | collective-permute-start | bytes 368648 | tf_op jit(solution)/shard_map/ppermute | solution.py:443
  31.1 7.6 %collective-permute-start.10 = (f32[5,2,40,128]{3,2,1,0:T(8,128)S(1)}, f32[5,2,40,128]{3,2,1,0:T(8,128)S(1)}, u32[]{:S(2)}, u32[]{:S(2)}) collective-permute-start(f32[5,2,40,128]{3,2,1,0:T(8,128)S(1)} %get-tuple-element.42), channel_id=1, source_target_pairs={{0,8},{8,0},{16,24},{24,16},{1,9},{9,1},{17,25},{25,17},{2,10},{10... | collective-permute-start | bytes 614408 | tf_op jit(solution)/shard_map/ppermute | solution.py:443
  32.6 7.4 %collective-permute-start.12 = (f32[5,2,40,128]{3,2,1,0:T(8,128)S(1)}, f32[5,2,40,128]{3,2,1,0:T(8,128)S(1)}, u32[]{:S(2)}, u32[]{:S(2)}) collective-permute-start(f32[5,2,40,128]{3,2,1,0:T(8,128)S(1)} %shard_map.126.order), channel_id=1, source_target_pairs={{0,16},{8,24},{16,0},{24,8},{1,17},{9,25},{17,1},{25,9},{2,18},{10... | collective-permute-start | bytes 614408 | tf_op jit(solution)/shard_map/ppermute | solution.py:443
  34.0 6.0 %collective-permute-start.14 = (f32[5,2,24,128]{3,2,1,0:T(8,128)S(1)}, f32[5,2,24,128]{3,2,1,0:T(8,128)S(1)}, u32[]{:S(2)}, u32[]{:S(2)}) collective-permute-start(f32[5,2,24,128]{3,2,1,0:T(8,128)S(1)} %shard_map.127), channel_id=1, source_target_pairs={{0,8},{8,0},{16,24},{24,16},{1,9},{9,1},{17,25},{25,17},{2,10},{10... | collective-permute-start | bytes 368648 | tf_op jit(solution)/shard_map/ppermute | solution.py:443
  (1 other events, 0.7 us)
where the time goes:
time: 41 us; the launch traced here: 40.7 us
  starting transfers between devices  25.8 us (63%)
  Pallas kernels  7.47 us (18%)
  waiting for transfers between devices  5.47 us (13%)
  local copies, waits for them, and re-layouts  1.14 us (3%)
  between operations  0.87 us (2%)
    ppermute x9, starting transfers between devices, swap(): lax.ppermute(values, 'shot', [(index, index ^ member) for index in range(...  13 us
    ppermute x6, starting transfers between devices, pair(): lax.ppermute(values, 'domain', pairs + [(target, source) for source, targ...  12.8 us
    pallas_call x20, Pallas kernels, call(): pl.pallas_call(kernel, out_shape=outs, in_specs=[VMEM] * len(operands), o...  7.47 us
    ppermute x9, waiting for transfers between devices, swap(): lax.ppermute(values, 'shot', [(index, index ^ member) for index in range(...  5.45 us
    unnamed x20, local copies, waits for them, and re-layouts  1.14 us
  transfers between devices with their start and end apart: 15, of which 5 were waited for; matrix products, arithmetic and copies ran while one was open for 0% of the time, Pallas kernels for 16%

commit v1 on v0

--- a/solution.py
+++ b/solution.py
@@ -255,7 +255,7 @@
         inner, outer, table, _, _, late, padded = refs
         fill_padded(padded, adjoint, inner, outer, 2)
     else:
-        padded, table, late = refs
+        padded, table, *_, late = refs
     depth, width, length = adjoint.shape[1:]
     quarter = width // shots
     lane = lax.broadcasted_iota(jnp.int32, (depth, ROWS, length), 2)
@@ -495,19 +495,19 @@
         after, inner, outer, table, outer_near, inner_near,
     )
 
-    def late_of(member):
+    def late_of(member, order=()):
         if member == last:
             return late_last
         return call(
-            functools.partial(backward_kernel, shots, member, False), [late_shape], 0.6, after, ring, table
+            functools.partial(backward_kernel, shots, member, False), [late_shape], 0.6, after, ring, table, *order
         )[0]
 
-    def image(member, parts=(0, 1), came=(), order=()):
+    def image(member, parts=(0, 1), came=(), order=(), late_order=()):
         rest_edges = (outer_rest, inner_rest) if 1 in parts else ()
         return call(
             functools.partial(image_kernel, shots, member, cut, parts, bool(order)), [piece_shapes[part] for part in parts], 1.2,
             cells, spot, wave, before, after, fields, outer_near, inner_near, *order, *rest_edges,
-            table, terms, late_of(member), hits, sums, *came,
+            table, terms, late_of(member, late_order), hits, sums, *came,
             scratch=[pltpu.VMEM((2, depth + 2, quarter + 2 * PAD, length), jnp.float32)],
         )
 
@@ -518,7 +518,7 @@
         from_y = swap(far_second, 2)
         y_first, y_second = image(2, order=(far_second,))
         near_y = swap(y_second, 2)
-        x_first, x_second = image(1, order=(y_second,))
+        x_first, x_second = image(1, order=(y_second,), late_order=(y_second,))
         near_x = swap(x_first, 1)
         (y_first,) = call(add_kernel, piece_shapes[:1], 0.1, y_first, from_x, far_first)
         over_y = swap(y_first, 2)

time: 41 us -> 41.3 us (level)
  no operation moved by 1% of the time
where the time goes in v1:
time: 41.3 us; the launch traced here: 41.1 us
  starting transfers between devices  25.8 us (62%)
  Pallas kernels  7.48 us (18%)
  waiting for transfers between devices  5.81 us (14%)
  local copies, waits for them, and re-layouts  1.14 us (3%)
  between operations  0.87 us (2%)
    ppermute x9, starting transfers between devices, swap(): lax.ppermute(values, 'shot', [(index, index ^ member) for index in range(...  13 us
    ppermute x6, starting transfers between devices, pair(): lax.ppermute(values, 'domain', pairs + [(target, source) for source, targ...  12.8 us
    pallas_call x20, Pallas kernels, call(): pl.pallas_call(kernel, out_shape=outs, in_specs=[VMEM] * len(operands), o...  7.48 us
    ppermute x9, waiting for transfers between devices, swap(): lax.ppermute(values, 'shot', [(index, index ^ member) for index in range(...  5.79 us
    unnamed x20, local copies, waits for them, and re-layouts  1.14 us
  transfers between devices with their start and end apart: 15, of which 5 were waited for; matrix products, arithmetic and copies ran while one was open for 0% of the time, Pallas kernels for 16%

profile of v1, /device:TPU:0, one launch (start us, length us, event | category | flops | bytes accessed | tf_op | source)
XLA Modules:
  0.0 41.1 jit_solution(5713311637288007082)
XLA Ops:
  0.2 0.6 %copy-done.7 = f32[2,64,128]{2,1,0:T(8,128)S(1)} copy-done((f32[2,64,128]{2,1,0:T(8,128)S(1)}, f32[2,64,128]{2,1,0:T(8,128)}, u32[]{:S(2)}) %copy-start.7) | copy-done | bytes 65560
  1.0 4.0 %collective-permute-start.2 = (f32[5,2,64,128]{3,2,1,0:T(8,128)S(1)}, f32[5,2,64,128]{3,2,1,0:T(8,128)S(1)}, u32[]{:S(2)}, u32[]{:S(2)}) collective-permute-start(f32[5,2,64,128]{3,2,1,0:T(8,128)S(1)} %shard_map.110.refs_0_.order), channel_id=1, source_target_pairs={{0,24},{8,16},{16,8},{24,0},{1,25},{9,17},{17,9},{25,1},{2,26},{10... | collective-permute-start | bytes 983048 | tf_op jit(solution)/shard_map/ppermute | solution.py:443
  5.0 0.7 %collective-permute-start.3 = (f32[4,256,128]{2,1,0:T(8,128)S(1)}, f32[4,256,128]{2,1,0:T(8,128)S(1)}, u32[]{:S(2)}, u32[]{:S(2)}) collective-permute-start(f32[4,256,128]{2,1,0:T(8,128)S(1)} %get-tuple-element.26), channel_id=1, source_target_pairs={{1,2},{3,4},{5,6},{2,1},{4,3},{6,5},{9,10},{11,12},{13,14},{10,9},... | collective-permute-start | bytes 1572872 | tf_op jit(solution)/shard_map/ppermute | solution.py:447
  5.7 3.0 %collective-permute-start.4 = (f32[4,256,128]{2,1,0:T(8,128)S(1)}, f32[4,256,128]{2,1,0:T(8,128)S(1)}, u32[]{:S(2)}, u32[]{:S(2)}) collective-permute-start(f32[4,256,128]{2,1,0:T(8,128)S(1)} %get-tuple-element.27), channel_id=1, source_target_pairs={{0,1},{2,3},{4,5},{6,7},{1,0},{3,2},{5,4},{7,6},{8,9},{10,11},{12,... | collective-permute-start | bytes 1572872 | tf_op jit(solution)/shard_map/ppermute | solution.py:447
  9.2 1.3 %collective-permute-start = (f32[5,2,64,128]{3,2,1,0:T(8,128)S(1)}, f32[5,2,64,128]{3,2,1,0:T(8,128)S(1)}, u32[]{:S(2)}, u32[]{:S(2)}) collective-permute-start(f32[5,2,64,128]{3,2,1,0:T(8,128)S(1)} %shard_map.110.refs_0_.order), channel_id=1, source_target_pairs={{0,8},{8,0},{16,24},{24,16},{1,9},{9,1},{17,25},{25,17},{2,10},{10... | collective-permute-start | bytes 983048 | tf_op jit(solution)/shard_map/ppermute | solution.py:443
  11.1 0.7 %shard_map.111 = (f32[2,256,128]{2,1,0:T(8,128)S(1)}, f32[2,256,128]{2,1,0:T(8,128)S(1)}) custom-call(s32[1,256]{1,0:T(1,128)S(1)} %copy-done.9, f32[2,256]{1,0:T(2,128)S(1)} %bitcast.32), custom_call_target="tpu_custom_call" | custom-call | flops 1500000000 | bytes 527360 | tf_op jit(solution)/shard_map/pallas_call | solution.py:407
  11.8 1.3 %collective-permute-done.2.refs_1_ = f32[5,2,64,128]{3,2,1,0:T(8,128)S(1)} collective-permute-done((f32[5,2,64,128]{3,2,1,0:T(8,128)S(1)}, f32[5,2,64,128]{3,2,1,0:T(8,128)S(1)}, u32[]{:S(2)}, u32[]{:S(2)}) %collective-permute-start.2) | collective-permute-done | bytes 327712 | tf_op jit(solution)/shard_map/ppermute | solution.py:443
  13.7 0.8 %shard_map.114 = (f32[2,2,256,128]{3,2,1,0:T(8,128)S(1)}, f32[6,2,256,128]{3,2,1,0:T(8,128)S(1)}, f32[2,128,128]{2,1,0:T(8,128)S(1)}, f32[2,128,128]{2,1,0:T(8,128)S(1)}, f32[2,4,272,128]{3,2,1,0:T(8,128)S(1)}) custom-call(s32[2,256,128]{2,1,0:T(8,128)S(1)} %shard_map.109.order.cells, s32[1,1]{1,0:T(1,128)} %bitcast.4.source, f32[1,2]{1,0:T(1,128)S(1)} %copy-done.2, ...), custom_call_target="tpu_custom_call" | custom-call | flops 1200000000 | bytes 7667724 | tf_op jit(solution)/shard_map/pallas_call | solution.py:407
  14.6 0.7 %collective-permute-start.5 = (f32[2,128,128]{2,1,0:T(8,128)S(1)}, f32[2,128,128]{2,1,0:T(8,128)S(1)}, u32[]{:S(2)}, u32[]{:S(2)}) collective-permute-start(f32[2,128,128]{2,1,0:T(8,128)S(1)} %get-tuple-element.32), channel_id=1, source_target_pairs={{1,2},{3,4},{5,6},{2,1},{4,3},{6,5},{9,10},{11,12},{13,14},{10,9},... | collective-permute-start | bytes 393224 | tf_op jit(solution)/shard_map/ppermute | solution.py:447
  15.3 4.8 %collective-permute-start.6 = (f32[2,128,128]{2,1,0:T(8,128)S(1)}, f32[2,128,128]{2,1,0:T(8,128)S(1)}, u32[]{:S(2)}, u32[]{:S(2)}) collective-permute-start(f32[2,128,128]{2,1,0:T(8,128)S(1)} %get-tuple-element.33), channel_id=1, source_target_pairs={{0,1},{2,3},{4,5},{6,7},{1,0},{3,2},{5,4},{7,6},{8,9},{10,11},{12,... | collective-permute-start | bytes 393224 | tf_op jit(solution)/shard_map/ppermute | solution.py:447
  20.1 0.9 %shard_map.115 = (f32[7,2,256,128]{3,2,1,0:T(8,128)S(1)}, f32[2,2,256,128]{3,2,1,0:T(8,128)S(1)}, f32[6,2,256,128]{3,2,1,0:T(8,128)S(1)}, f32[2,128,128]{2,1,0:T(8,128)S(1)}, f32[2,128,128]{2,1,0:T(8,128)S(1)}) custom-call(s32[2,256,128]{2,1,0:T(8,128)S(1)} %shard_map.109.order.cells, ...), custom_call_target="tpu_custom_call", output_to_operand_aliasing={{0}: (7, {}), {1}: (8, {}), {2}: (9, {})} | custom-call | flops 1200000000 | bytes 11206668 | tf_op jit(solution)/shard_map/pallas_call | solution.py:407
  21.0 0.7 %collective-permute-start.7 = (f32[2,128,128]{2,1,0:T(8,128)S(1)}, f32[2,128,128]{2,1,0:T(8,128)S(1)}, u32[]{:S(2)}, u32[]{:S(2)}) collective-permute-start(f32[2,128,128]{2,1,0:T(8,128)S(1)} %get-tuple-element.34), channel_id=1, source_target_pairs={{1,2},{3,4},{5,6},{2,1},{4,3},{6,5},{9,10},{11,12},{13,14},{10,9},... | collective-permute-start | bytes 393224 | tf_op jit(solution)/shard_map/ppermute | solution.py:447
  21.7 3.0 %collective-permute-start.8 = (f32[2,128,128]{2,1,0:T(8,128)S(1)}, f32[2,128,128]{2,1,0:T(8,128)S(1)}, u32[]{:S(2)}, u32[]{:S(2)}) collective-permute-start(f32[2,128,128]{2,1,0:T(8,128)S(1)} %get-tuple-element.35), channel_id=1, source_target_pairs={{0,1},{2,3},{4,5},{6,7},{1,0},{3,2},{5,4},{7,6},{8,9},{10,11},{12,... | collective-permute-start | bytes 393224 | tf_op jit(solution)/shard_map/ppermute | solution.py:447
  25.5 1.4 %collective-permute-start.11 = (f32[5,2,40,128]{3,2,1,0:T(8,128)S(1)}, f32[5,2,40,128]{3,2,1,0:T(8,128)S(1)}, u32[]{:S(2)}, u32[]{:S(2)}) collective-permute-start(f32[5,2,40,128]{3,2,1,0:T(8,128)S(1)} %shard_map.118.refs_0_.order), channel_id=1, source_target_pairs={{0,8},{8,0},{16,24},{24,16},{1,9},{9,1},{17,25},{25,17},{2,10},{10... | collective-permute-start | bytes 614408 | tf_op jit(solution)/shard_map/ppermute | solution.py:443
  27.5 1.5 %collective-permute-start.13 = (f32[5,2,24,128]{3,2,1,0:T(8,128)S(1)}, f32[5,2,24,128]{3,2,1,0:T(8,128)S(1)}, u32[]{:S(2)}, u32[]{:S(2)}) collective-permute-start(f32[5,2,24,128]{3,2,1,0:T(8,128)S(1)} %shard_map.119.refs_0_), channel_id=1, source_target_pairs={{0,16},{8,24},{16,0},{24,8},{1,17},{9,25},{17,1},{25,9},{2,18},{10... | collective-permute-start | bytes 368648 | tf_op jit(solution)/shard_map/ppermute | solution.py:443
  29.0 0.5 %shard_map.121 = (f32[5,2,40,128]{3,2,1,0:T(8,128)S(1)}, f32[5,2,24,128]{3,2,1,0:T(8,128)S(1)}) custom-call(s32[2,256,128]{2,1,0:T(8,128)S(1)} %shard_map.109.order.cells, s32[1,1]{1,0:T(1,128)} %bitcast.8.source, f32[1,2]{1,0:T(1,128)S(1)} %copy-done.2, f32[4,2,256,128]{3,2,1,0:T(8,128)S(1)} %bitcast.28, f32[4,2,256,128]{3,2,1,0:T(8,128)S(1)} %bitcast.17, ...), custom_call_target="tpu_custom_call" | custom-call | flops 1200000000 | bytes 7921676 | tf_op jit(solution)/shard_map/pallas_call | solution.py:407
  29.9 0.6 %collective-permute-start.9 = (f32[5,2,24,128]{3,2,1,0:T(8,128)S(1)}, f32[5,2,24,128]{3,2,1,0:T(8,128)S(1)}, u32[]{:S(2)}, u32[]{:S(2)}) collective-permute-start(f32[5,2,24,128]{3,2,1,0:T(8,128)S(1)} %get-tuple-element.41.refs_2_.refs_0_), channel_id=1, source_target_pairs={{0,16},{8,24},{16,0},{24,8},{1,17},{9,25},{17,1},{25,9},{2,18},{10... | collective-permute-start | bytes 368648 | tf_op jit(solution)/shard_map/ppermute | solution.py:443
  31.1 0.7 %collective-permute-start.10 = (f32[5,2,40,128]{3,2,1,0:T(8,128)S(1)}, f32[5,2,40,128]{3,2,1,0:T(8,128)S(1)}, u32[]{:S(2)}, u32[]{:S(2)}) collective-permute-start(f32[5,2,40,128]{3,2,1,0:T(8,128)S(1)} %get-tuple-element.42), channel_id=1, source_target_pairs={{0,8},{8,0},{16,24},{24,16},{1,9},{9,1},{17,25},{25,17},{2,10},{10... | collective-permute-start | bytes 614408 | tf_op jit(solution)/shard_map/ppermute | solution.py:443
  32.6 1.4 %collective-permute-start.12 = (f32[5,2,40,128]{3,2,1,0:T(8,128)S(1)}, f32[5,2,40,128]{3,2,1,0:T(8,128)S(1)}, u32[]{:S(2)}, u32[]{:S(2)}) collective-permute-start(f32[5,2,40,128]{3,2,1,0:T(8,128)S(1)} %shard_map.126.order), channel_id=1, source_target_pairs={{0,16},{8,24},{16,0},{24,8},{1,17},{9,25},{17,1},{25,9},{2,18},{10... | collective-permute-start | bytes 614408 | tf_op jit(solution)/shard_map/ppermute | solution.py:443
  34.0 1.6 %collective-permute-start.14 = (f32[5,2,24,128]{3,2,1,0:T(8,128)S(1)}, f32[5,2,24,128]{3,2,1,0:T(8,128)S(1)}, u32[]{:S(2)}, u32[]{:S(2)}) collective-permute-start(f32[5,2,24,128]{3,2,1,0:T(8,128)S(1)} %shard_map.127), channel_id=1, source_target_pairs={{0,8},{8,0},{16,24},{24,16},{1,9},{9,1},{17,25},{25,17},{2,10},{10... | collective-permute-start | bytes 368648 | tf_op jit(solution)/shard_map/ppermute | solution.py:443
  35.6 0.7 %collective-permute-done.9.refs_7_ = f32[5,2,24,128]{3,2,1,0:T(8,128)S(1)} collective-permute-done((f32[5,2,24,128]{3,2,1,0:T(8,128)S(1)}, f32[5,2,24,128]{3,2,1,0:T(8,128)S(1)}, u32[]{:S(2)}, u32[]{:S(2)}) %collective-permute-start.9) | collective-permute-done | bytes 122912 | tf_op jit(solution)/shard_map/ppermute | solution.py:443
  36.5 2.5 %collective-permute-done.10.refs_6_ = f32[5,2,40,128]{3,2,1,0:T(8,128)S(1)} collective-permute-done((f32[5,2,40,128]{3,2,1,0:T(8,128)S(1)}, f32[5,2,40,128]{3,2,1,0:T(8,128)S(1)}, u32[]{:S(2)}, u32[]{:S(2)}) %collective-permute-start.10) | collective-permute-done | bytes 204832 | tf_op jit(solution)/shard_map/ppermute | solution.py:443
  39.4 0.9 %collective-permute-done.14.refs_3_ = f32[5,2,24,128]{3,2,1,0:T(8,128)S(1)} collective-permute-done((f32[5,2,24,128]{3,2,1,0:T(8,128)S(1)}, f32[5,2,24,128]{3,2,1,0:T(8,128)S(1)}, u32[]{:S(2)}, u32[]{:S(2)}) %collective-permute-start.14) | collective-permute-done | bytes 122912 | tf_op jit(solution)/shard_map/ppermute | solution.py:443
  40.3 0.8 %shard_map.128 = f32[5,2,64,128]{3,2,1,0:T(8,128)} custom-call(f32[5,2,40,128]{3,2,1,0:T(8,128)S(1)} %shard_map.125.refs_0_, f32[5,2,40,128]{3,2,1,0:T(8,128)S(1)} %collective-permute-done.12.refs_1_, f32[5,2,24,128]{3,2,1,0:T(8,128)S(1)} %shard_map.122.refs_0_.refs_2_, f32[5,2,24,128]{3,2,1,0:T(8,128)S(1)} %collective-permute-done.14.refs_3_), custom_call_target="tpu_custom_call" | custom-call | flops 800000000 | bytes 983040 | tf_op jit(solution)/shard_map/pallas_call | solution.py:407
  (46 shorter events, 5.2 us)
Async XLA Ops:
  0.0 0.8 %copy-start.7 = (f32[2,64,128]{2,1,0:T(8,128)S(1)}, f32[2,64,128]{2,1,0:T(8,128)}, u32[]{:S(2)}) copy-start(f32[2,64,128]{2,1,0:T(8,128)} %refs_4_.1) | copy-start | bytes 196612
  0.0 0.9 %copy-start.6 = (f32[2,64,128]{2,1,0:T(8,128)S(1)}, f32[2,64,128]{2,1,0:T(8,128)}, u32[]{:S(2)}) copy-start(f32[2,64,128]{2,1,0:T(8,128)} %refs_3_.1) | copy-start | bytes 196612
  0.0 0.9 %copy-start.5 = (f32[2,64,128]{2,1,0:T(8,128)S(1)}, f32[2,64,128]{2,1,0:T(8,128)}, u32[]{:S(2)}) copy-start(f32[2,64,128]{2,1,0:T(8,128)} %refs_2_.1) | copy-start | bytes 196612
  0.0 0.9 %copy-start.4 = (f32[2,64,128]{2,1,0:T(8,128)S(1)}, f32[2,64,128]{2,1,0:T(8,128)}, u32[]{:S(2)}) copy-start(f32[2,64,128]{2,1,0:T(8,128)} %refs_1_.1) | copy-start | bytes 196612
  0.0 1.0 %copy-start.3 = (f32[2,64,128]{2,1,0:T(8,128)S(1)}, f32[2,64,128]{2,1,0:T(8,128)}, u32[]{:S(2)}) copy-start(f32[2,64,128]{2,1,0:T(8,128)} %refs_0_.1) | copy-start | bytes 196612
  0.0 4.9 %copy-start.1 = (f32[1,4,2,256,128]{4,3,2,1,0:T(8,128)S(1)}, f32[1,4,2,256,128]{4,3,2,1,0:T(8,128)}, u32[]{:S(2)}) copy-start(f32[1,4,2,256,128]{4,3,2,1,0:T(8,128)} %param.16) | copy-start | bytes 3145732
  1.0 4.0 %copy-start = (f32[1,4,2,256,128]{4,3,2,1,0:T(8,128)S(1)}, f32[1,4,2,256,128]{4,3,2,1,0:T(8,128)}, u32[]{:S(2)}) copy-start(f32[1,4,2,256,128]{4,3,2,1,0:T(8,128)} %param.17) | copy-start | bytes 3145732
  1.0 10.2 %copy-start.8 = (f32[1,2,256]{2,1,0:T(2,128)S(1)}, f32[1,2,256]{2,1,0:T(2,128)}, u32[]{:S(2)}) copy-start(f32[1,2,256]{2,1,0:T(2,128)} %param.21) | copy-start | bytes 6148
  1.0 10.2 %copy-start.9 = (s32[1,256]{1,0:T(1,128)S(1)}, s32[1,256]{1,0:T(1,128)}, u32[]{:S(2)}) copy-start(s32[1,256]{1,0:T(1,128)} %receivers.1) | copy-start | bytes 3076
  1.0 12.1 %collective-permute-start.2 = (f32[5,2,64,128]{3,2,1,0:T(8,128)S(1)}, f32[5,2,64,128]{3,2,1,0:T(8,128)S(1)}, u32[]{:S(2)}, u32[]{:S(2)}) collective-permute-start(f32[5,2,64,128]{3,2,1,0:T(8,128)S(1)} %shard_map.110.refs_0_.order), channel_id=1, source_target_pairs={{0,24},{8,16},{16,8},{24,0},{1,25},{9,17},{17,9},{25,1},{2,26},{10... | collective-permute-start | bytes 983048 | tf_op jit(solution)/shard_map/ppermute | solution.py:443
  5.0 8.3 %collective-permute-start.3 = (f32[4,256,128]{2,1,0:T(8,128)S(1)}, f32[4,256,128]{2,1,0:T(8,128)S(1)}, u32[]{:S(2)}, u32[]{:S(2)}) collective-permute-start(f32[4,256,128]{2,1,0:T(8,128)S(1)} %get-tuple-element.26), channel_id=1, source_target_pairs={{1,2},{3,4},{5,6},{2,1},{4,3},{6,5},{9,10},{11,12},{13,14},{10,9},... | collective-permute-start | bytes 1572872 | tf_op jit(solution)/shard_map/ppermute | solution.py:447
  5.7 7.7 %collective-permute-start.4 = (f32[4,256,128]{2,1,0:T(8,128)S(1)}, f32[4,256,128]{2,1,0:T(8,128)S(1)}, u32[]{:S(2)}, u32[]{:S(2)}) collective-permute-start(f32[4,256,128]{2,1,0:T(8,128)S(1)} %get-tuple-element.27), channel_id=1, source_target_pairs={{0,1},{2,3},{4,5},{6,7},{1,0},{3,2},{5,4},{7,6},{8,9},{10,11},{12,... | collective-permute-start | bytes 1572872 | tf_op jit(solution)/shard_map/ppermute | solution.py:447
  8.7 11.4 %collective-permute-start.1 = (f32[5,2,64,128]{3,2,1,0:T(8,128)S(1)}, f32[5,2,64,128]{3,2,1,0:T(8,128)S(1)}, u32[]{:S(2)}, u32[]{:S(2)}) collective-permute-start(f32[5,2,64,128]{3,2,1,0:T(8,128)S(1)} %shard_map.110.refs_0_.order), channel_id=1, source_target_pairs={{0,16},{8,24},{16,0},{24,8},{1,17},{9,25},{17,1},{25,9},{2,18},{10... | collective-permute-start | bytes 983048 | tf_op jit(solution)/shard_map/ppermute | solution.py:443
  9.2 10.9 %collective-permute-start = (f32[5,2,64,128]{3,2,1,0:T(8,128)S(1)}, f32[5,2,64,128]{3,2,1,0:T(8,128)S(1)}, u32[]{:S(2)}, u32[]{:S(2)}) collective-permute-start(f32[5,2,64,128]{3,2,1,0:T(8,128)S(1)} %shard_map.110.refs_0_.order), channel_id=1, source_target_pairs={{0,8},{8,0},{16,24},{24,16},{1,9},{9,1},{17,25},{25,17},{2,10},{10... | collective-permute-start | bytes 983048 | tf_op jit(solution)/shard_map/ppermute | solution.py:443
  14.6 10.1 %collective-permute-start.5 = (f32[2,128,128]{2,1,0:T(8,128)S(1)}, f32[2,128,128]{2,1,0:T(8,128)S(1)}, u32[]{:S(2)}, u32[]{:S(2)}) collective-permute-start(f32[2,128,128]{2,1,0:T(8,128)S(1)} %get-tuple-element.32), channel_id=1, source_target_pairs={{1,2},{3,4},{5,6},{2,1},{4,3},{6,5},{9,10},{11,12},{13,14},{10,9},... | collective-permute-start | bytes 393224 | tf_op jit(solution)/shard_map/ppermute | solution.py:447
  15.3 9.4 %collective-permute-start.6 = (f32[2,128,128]{2,1,0:T(8,128)S(1)}, f32[2,128,128]{2,1,0:T(8,128)S(1)}, u32[]{:S(2)}, u32[]{:S(2)}) collective-permute-start(f32[2,128,128]{2,1,0:T(8,128)S(1)} %get-tuple-element.33), channel_id=1, source_target_pairs={{0,1},{2,3},{4,5},{6,7},{1,0},{3,2},{5,4},{7,6},{8,9},{10,11},{12,... | collective-permute-start | bytes 393224 | tf_op jit(solution)/shard_map/ppermute | solution.py:447
  21.0 6.2 %collective-permute-start.7 = (f32[2,128,128]{2,1,0:T(8,128)S(1)}, f32[2,128,128]{2,1,0:T(8,128)S(1)}, u32[]{:S(2)}, u32[]{:S(2)}) collective-permute-start(f32[2,128,128]{2,1,0:T(8,128)S(1)} %get-tuple-element.34), channel_id=1, source_target_pairs={{1,2},{3,4},{5,6},{2,1},{4,3},{6,5},{9,10},{11,12},{13,14},{10,9},... | collective-permute-start | bytes 393224 | tf_op jit(solution)/shard_map/ppermute | solution.py:447
  21.7 5.5 %collective-permute-start.8 = (f32[2,128,128]{2,1,0:T(8,128)S(1)}, f32[2,128,128]{2,1,0:T(8,128)S(1)}, u32[]{:S(2)}, u32[]{:S(2)}) collective-permute-start(f32[2,128,128]{2,1,0:T(8,128)S(1)} %get-tuple-element.35), channel_id=1, source_target_pairs={{0,1},{2,3},{4,5},{6,7},{1,0},{3,2},{5,4},{7,6},{8,9},{10,11},{12,... | collective-permute-start | bytes 393224 | tf_op jit(solution)/shard_map/ppermute | solution.py:447
  25.5 7.1 %collective-permute-start.11 = (f32[5,2,40,128]{3,2,1,0:T(8,128)S(1)}, f32[5,2,40,128]{3,2,1,0:T(8,128)S(1)}, u32[]{:S(2)}, u32[]{:S(2)}) collective-permute-start(f32[5,2,40,128]{3,2,1,0:T(8,128)S(1)} %shard_map.118.refs_0_.order), channel_id=1, source_target_pairs={{0,8},{8,0},{16,24},{24,16},{1,9},{9,1},{17,25},{25,17},{2,10},{10... | collective-permute-start | bytes 614408 | tf_op jit(solution)/shard_map/ppermute | solution.py:443
  27.5 6.5 %collective-permute-start.13 = (f32[5,2,24,128]{3,2,1,0:T(8,128)S(1)}, f32[5,2,24,128]{3,2,1,0:T(8,128)S(1)}, u32[]{:S(2)}, u32[]{:S(2)}) collective-permute-start(f32[5,2,24,128]{3,2,1,0:T(8,128)S(1)} %shard_map.119.refs_0_), channel_id=1, source_target_pairs={{0,16},{8,24},{16,0},{24,8},{1,17},{9,25},{17,1},{25,9},{2,18},{10... | collective-permute-start | bytes 368648 | tf_op jit(solution)/shard_map/ppermute | solution.py:443
  29.9 6.3 %collective-permute-start.9 = (f32[5,2,24,128]{3,2,1,0:T(8,128)S(1)}, f32[5,2,24,128]{3,2,1,0:T(8,128)S(1)}, u32[]{:S(2)}, u32[]{:S(2)}) collective-permute-start(f32[5,2,24,128]{3,2,1,0:T(8,128)S(1)} %get-tuple-element.41.refs_2_.refs_0_), channel_id=1, source_target_pairs={{0,16},{8,24},{16,0},{24,8},{1,17},{9,25},{17,1},{25,9},{2,18},{10... | collective-permute-start | bytes 368648 | tf_op jit(solution)/shard_map/ppermute | solution.py:443
  31.1 7.9 %collective-permute-start.10 = (f32[5,2,40,128]{3,2,1,0:T(8,128)S(1)}, f32[5,2,40,128]{3,2,1,0:T(8,128)S(1)}, u32[]{:S(2)}, u32[]{:S(2)}) collective-permute-start(f32[5,2,40,128]{3,2,1,0:T(8,128)S(1)} %get-tuple-element.42), channel_id=1, source_target_pairs={{0,8},{8,0},{16,24},{24,16},{1,9},{9,1},{17,25},{25,17},{2,10},{10... | collective-permute-start | bytes 614408 | tf_op jit(solution)/shard_map/ppermute | solution.py:443
  32.6 7.7 %collective-permute-start.12 = (f32[5,2,40,128]{3,2,1,0:T(8,128)S(1)}, f32[5,2,40,128]{3,2,1,0:T(8,128)S(1)}, u32[]{:S(2)}, u32[]{:S(2)}) collective-permute-start(f32[5,2,40,128]{3,2,1,0:T(8,128)S(1)} %shard_map.126.order), channel_id=1, source_target_pairs={{0,16},{8,24},{16,0},{24,8},{1,17},{9,25},{17,1},{25,9},{2,18},{10... | collective-permute-start | bytes 614408 | tf_op jit(solution)/shard_map/ppermute | solution.py:443
  34.0 6.3 %collective-permute-start.14 = (f32[5,2,24,128]{3,2,1,0:T(8,128)S(1)}, f32[5,2,24,128]{3,2,1,0:T(8,128)S(1)}, u32[]{:S(2)}, u32[]{:S(2)}) collective-permute-start(f32[5,2,24,128]{3,2,1,0:T(8,128)S(1)} %shard_map.127), channel_id=1, source_target_pairs={{0,8},{8,0},{16,24},{24,16},{1,9},{9,1},{17,25},{25,17},{2,10},{10... | collective-permute-start | bytes 368648 | tf_op jit(solution)/shard_map/ppermute | solution.py:443
  (1 other events, 0.7 us)

commit v2 on v0

--- a/solution.py
+++ b/solution.py
@@ -9,7 +9,7 @@
 from jax.sharding import PartitionSpec as P
 
 STEPS = 2
-ROWS = 16
+ROWS = 32
 PAD = 8
 VMEM_LIMIT = 32 * 1024 * 1024
 FLOPS_PER_MICRO = 10**9

time: 41 us -> 41.2 us (level)
  transfers between devices with their start and end apart: 15 -> 15, of which waited for: 5 -> 5; matrix products, arithmetic and copies ran while one was open for 0% -> 0% of each run, Pallas kernels for 16% -> 17%
where the time goes in v2:
time: 41.2 us; the launch traced here: 41 us
  starting transfers between devices  25.7 us (62%)
  Pallas kernels  7.74 us (19%)
  waiting for transfers between devices  5.41 us (13%)
  local copies, waits for them, and re-layouts  1.21 us (3%)
  between operations  0.88 us (2%)
    ppermute x9, starting transfers between devices, swap(): lax.ppermute(values, 'shot', [(index, index ^ member) for index in range(...  12.9 us
    ppermute x6, starting transfers between devices, pair(): lax.ppermute(values, 'domain', pairs + [(target, source) for source, targ...  12.8 us
    pallas_call x20, Pallas kernels, call(): pl.pallas_call(kernel, out_shape=outs, in_specs=[VMEM] * len(operands), o...  7.74 us
    ppermute x9, waiting for transfers between devices, swap(): lax.ppermute(values, 'shot', [(index, index ^ member) for index in range(...  5.39 us
    unnamed x20, local copies, waits for them, and re-layouts  1.21 us
  transfers between devices with their start and end apart: 15, of which 5 were waited for; matrix products, arithmetic and copies ran while one was open for 0% of the time, Pallas kernels for 17%

profile of v2, /device:TPU:0, one launch (start us, length us, event | category | flops | bytes accessed | tf_op | source)
XLA Modules:
  0.0 41.0 jit_solution(16352851137310221222)
XLA Ops:
  0.1 0.7 %copy-done.7 = f32[2,64,128]{2,1,0:T(8,128)S(1)} copy-done((f32[2,64,128]{2,1,0:T(8,128)S(1)}, f32[2,64,128]{2,1,0:T(8,128)}, u32[]{:S(2)}) %copy-start.7) | copy-done | bytes 65560
  1.0 4.0 %collective-permute-start.2 = (f32[5,2,64,128]{3,2,1,0:T(8,128)S(1)}, f32[5,2,64,128]{3,2,1,0:T(8,128)S(1)}, u32[]{:S(2)}, u32[]{:S(2)}) collective-permute-start(f32[5,2,64,128]{3,2,1,0:T(8,128)S(1)} %shard_map.110.refs_0_.order), channel_id=1, source_target_pairs={{0,24},{8,16},{16,8},{24,0},{1,25},{9,17},{17,9},{25,1},{2,26},{10... | collective-permute-start | bytes 983048 | tf_op jit(solution)/shard_map/ppermute | solution.py:443
  5.0 0.7 %collective-permute-start.3 = (f32[4,256,128]{2,1,0:T(8,128)S(1)}, f32[4,256,128]{2,1,0:T(8,128)S(1)}, u32[]{:S(2)}, u32[]{:S(2)}) collective-permute-start(f32[4,256,128]{2,1,0:T(8,128)S(1)} %get-tuple-element.26), channel_id=1, source_target_pairs={{1,2},{3,4},{5,6},{2,1},{4,3},{6,5},{9,10},{11,12},{13,14},{10,9},... | collective-permute-start | bytes 1572872 | tf_op jit(solution)/shard_map/ppermute | solution.py:447
  5.7 3.0 %collective-permute-start.4 = (f32[4,256,128]{2,1,0:T(8,128)S(1)}, f32[4,256,128]{2,1,0:T(8,128)S(1)}, u32[]{:S(2)}, u32[]{:S(2)}) collective-permute-start(f32[4,256,128]{2,1,0:T(8,128)S(1)} %get-tuple-element.27), channel_id=1, source_target_pairs={{0,1},{2,3},{4,5},{6,7},{1,0},{3,2},{5,4},{7,6},{8,9},{10,11},{12,... | collective-permute-start | bytes 1572872 | tf_op jit(solution)/shard_map/ppermute | solution.py:447
  9.2 1.3 %collective-permute-start = (f32[5,2,64,128]{3,2,1,0:T(8,128)S(1)}, f32[5,2,64,128]{3,2,1,0:T(8,128)S(1)}, u32[]{:S(2)}, u32[]{:S(2)}) collective-permute-start(f32[5,2,64,128]{3,2,1,0:T(8,128)S(1)} %shard_map.110.refs_0_.order), channel_id=1, source_target_pairs={{0,8},{8,0},{16,24},{24,16},{1,9},{9,1},{17,25},{25,17},{2,10},{10... | collective-permute-start | bytes 983048 | tf_op jit(solution)/shard_map/ppermute | solution.py:443
  11.1 0.7 %shard_map.111 = (f32[2,256,128]{2,1,0:T(8,128)S(1)}, f32[2,256,128]{2,1,0:T(8,128)S(1)}) custom-call(s32[1,256]{1,0:T(1,128)S(1)} %copy-done.9, f32[2,256]{1,0:T(2,128)S(1)} %bitcast.32), custom_call_target="tpu_custom_call" | custom-call | flops 1500000000 | bytes 527360 | tf_op jit(solution)/shard_map/pallas_call | solution.py:407
  11.8 1.3 %collective-permute-done.2.refs_1_ = f32[5,2,64,128]{3,2,1,0:T(8,128)S(1)} collective-permute-done((f32[5,2,64,128]{3,2,1,0:T(8,128)S(1)}, f32[5,2,64,128]{3,2,1,0:T(8,128)S(1)}, u32[]{:S(2)}, u32[]{:S(2)}) %collective-permute-start.2) | collective-permute-done | bytes 327712 | tf_op jit(solution)/shard_map/ppermute | solution.py:443
  13.7 0.9 %shard_map.114 = (f32[2,2,256,128]{3,2,1,0:T(8,128)S(1)}, f32[6,2,256,128]{3,2,1,0:T(8,128)S(1)}, f32[2,128,128]{2,1,0:T(8,128)S(1)}, f32[2,128,128]{2,1,0:T(8,128)S(1)}, f32[2,4,272,128]{3,2,1,0:T(8,128)S(1)}) custom-call(s32[2,256,128]{2,1,0:T(8,128)S(1)} %shard_map.109.order.cells, s32[1,1]{1,0:T(1,128)} %bitcast.4.source, f32[1,2]{1,0:T(1,128)S(1)} %copy-done.2, ...), custom_call_target="tpu_custom_call" | custom-call | flops 1200000000 | bytes 7667724 | tf_op jit(solution)/shard_map/pallas_call | solution.py:407
  14.7 0.7 %collective-permute-start.5 = (f32[2,128,128]{2,1,0:T(8,128)S(1)}, f32[2,128,128]{2,1,0:T(8,128)S(1)}, u32[]{:S(2)}, u32[]{:S(2)}) collective-permute-start(f32[2,128,128]{2,1,0:T(8,128)S(1)} %get-tuple-element.32), channel_id=1, source_target_pairs={{1,2},{3,4},{5,6},{2,1},{4,3},{6,5},{9,10},{11,12},{13,14},{10,9},... | collective-permute-start | bytes 393224 | tf_op jit(solution)/shard_map/ppermute | solution.py:447
  15.3 4.8 %collective-permute-start.6 = (f32[2,128,128]{2,1,0:T(8,128)S(1)}, f32[2,128,128]{2,1,0:T(8,128)S(1)}, u32[]{:S(2)}, u32[]{:S(2)}) collective-permute-start(f32[2,128,128]{2,1,0:T(8,128)S(1)} %get-tuple-element.33), channel_id=1, source_target_pairs={{0,1},{2,3},{4,5},{6,7},{1,0},{3,2},{5,4},{7,6},{8,9},{10,11},{12,... | collective-permute-start | bytes 393224 | tf_op jit(solution)/shard_map/ppermute | solution.py:447
  20.1 1.0 %shard_map.115 = (f32[7,2,256,128]{3,2,1,0:T(8,128)S(1)}, f32[2,2,256,128]{3,2,1,0:T(8,128)S(1)}, f32[6,2,256,128]{3,2,1,0:T(8,128)S(1)}, f32[2,128,128]{2,1,0:T(8,128)S(1)}, f32[2,128,128]{2,1,0:T(8,128)S(1)}) custom-call(s32[2,256,128]{2,1,0:T(8,128)S(1)} %shard_map.109.order.cells, ...), custom_call_target="tpu_custom_call", output_to_operand_aliasing={{0}: (7, {}), {1}: (8, {}), {2}: (9, {})} | custom-call | flops 1200000000 | bytes 11206668 | tf_op jit(solution)/shard_map/pallas_call | solution.py:407
  21.1 0.7 %collective-permute-start.7 = (f32[2,128,128]{2,1,0:T(8,128)S(1)}, f32[2,128,128]{2,1,0:T(8,128)S(1)}, u32[]{:S(2)}, u32[]{:S(2)}) collective-permute-start(f32[2,128,128]{2,1,0:T(8,128)S(1)} %get-tuple-element.34), channel_id=1, source_target_pairs={{1,2},{3,4},{5,6},{2,1},{4,3},{6,5},{9,10},{11,12},{13,14},{10,9},... | collective-permute-start | bytes 393224 | tf_op jit(solution)/shard_map/ppermute | solution.py:447
  21.8 3.0 %collective-permute-start.8 = (f32[2,128,128]{2,1,0:T(8,128)S(1)}, f32[2,128,128]{2,1,0:T(8,128)S(1)}, u32[]{:S(2)}, u32[]{:S(2)}) collective-permute-start(f32[2,128,128]{2,1,0:T(8,128)S(1)} %get-tuple-element.35), channel_id=1, source_target_pairs={{0,1},{2,3},{4,5},{6,7},{1,0},{3,2},{5,4},{7,6},{8,9},{10,11},{12,... | collective-permute-start | bytes 393224 | tf_op jit(solution)/shard_map/ppermute | solution.py:447
  25.6 1.4 %collective-permute-start.11 = (f32[5,2,40,128]{3,2,1,0:T(8,128)S(1)}, f32[5,2,40,128]{3,2,1,0:T(8,128)S(1)}, u32[]{:S(2)}, u32[]{:S(2)}) collective-permute-start(f32[5,2,40,128]{3,2,1,0:T(8,128)S(1)} %shard_map.118.refs_0_.order), channel_id=1, source_target_pairs={{0,8},{8,0},{16,24},{24,16},{1,9},{9,1},{17,25},{25,17},{2,10},{10... | collective-permute-start | bytes 614408 | tf_op jit(solution)/shard_map/ppermute | solution.py:443
  28.0 1.5 %collective-permute-start.13 = (f32[5,2,24,128]{3,2,1,0:T(8,128)S(1)}, f32[5,2,24,128]{3,2,1,0:T(8,128)S(1)}, u32[]{:S(2)}, u32[]{:S(2)}) collective-permute-start(f32[5,2,24,128]{3,2,1,0:T(8,128)S(1)} %shard_map.119.refs_0_), channel_id=1, source_target_pairs={{0,16},{8,24},{16,0},{24,8},{1,17},{9,25},{17,1},{25,9},{2,18},{10... | collective-permute-start | bytes 368648 | tf_op jit(solution)/shard_map/ppermute | solution.py:443
  30.1 0.6 %collective-permute-start.9 = (f32[5,2,24,128]{3,2,1,0:T(8,128)S(1)}, f32[5,2,24,128]{3,2,1,0:T(8,128)S(1)}, u32[]{:S(2)}, u32[]{:S(2)}) collective-permute-start(f32[5,2,24,128]{3,2,1,0:T(8,128)S(1)} %get-tuple-element.41.refs_0_), channel_id=1, source_target_pairs={{0,16},{8,24},{16,0},{24,8},{1,17},{9,25},{17,1},{25,9},{2,18},{10... | collective-permute-start | bytes 368648 | tf_op jit(solution)/shard_map/ppermute | solution.py:443
  30.7 0.6 %shard_map.124 = (f32[5,2,40,128]{3,2,1,0:T(8,128)S(1)}, f32[5,2,24,128]{3,2,1,0:T(8,128)S(1)}) custom-call(s32[2,256,128]{2,1,0:T(8,128)S(1)} %shard_map.109.order.cells, s32[1,1]{1,0:T(1,128)} %bitcast.10.source, f32[1,2]{1,0:T(1,128)S(1)} %copy-done.2, f32[4,2,256,128]{3,2,1,0:T(8,128)S(1)} %bitcast.29, f32[4,2,256,128]{3,2,1,0:T(8,128)S(1)} %bitcast.19, ...), custom_call_target="tpu_custom_call" | custom-call | flops 1200000000 | bytes 7921676 | tf_op jit(solution)/shard_map/pallas_call | solution.py:407
  31.3 0.8 %collective-permute-start.10 = (f32[5,2,40,128]{3,2,1,0:T(8,128)S(1)}, f32[5,2,40,128]{3,2,1,0:T(8,128)S(1)}, u32[]{:S(2)}, u32[]{:S(2)}) collective-permute-start(f32[5,2,40,128]{3,2,1,0:T(8,128)S(1)} %get-tuple-element.42), channel_id=1, source_target_pairs={{0,8},{8,0},{16,24},{24,16},{1,9},{9,1},{17,25},{25,17},{2,10},{10... | collective-permute-start | bytes 614408 | tf_op jit(solution)/shard_map/ppermute | solution.py:443
  32.7 1.3 %collective-permute-start.12 = (f32[5,2,40,128]{3,2,1,0:T(8,128)S(1)}, f32[5,2,40,128]{3,2,1,0:T(8,128)S(1)}, u32[]{:S(2)}, u32[]{:S(2)}) collective-permute-start(f32[5,2,40,128]{3,2,1,0:T(8,128)S(1)} %shard_map.126.order), channel_id=1, source_target_pairs={{0,16},{8,24},{16,0},{24,8},{1,17},{9,25},{17,1},{25,9},{2,18},{10... | collective-permute-start | bytes 614408 | tf_op jit(solution)/shard_map/ppermute | solution.py:443
  34.1 1.6 %collective-permute-start.14 = (f32[5,2,24,128]{3,2,1,0:T(8,128)S(1)}, f32[5,2,24,128]{3,2,1,0:T(8,128)S(1)}, u32[]{:S(2)}, u32[]{:S(2)}) collective-permute-start(f32[5,2,24,128]{3,2,1,0:T(8,128)S(1)} %shard_map.127), channel_id=1, source_target_pairs={{0,8},{8,0},{16,24},{24,16},{1,9},{9,1},{17,25},{25,17},{2,10},{10... | collective-permute-start | bytes 368648 | tf_op jit(solution)/shard_map/ppermute | solution.py:443
  35.6 0.9 %collective-permute-done.9.refs_7_ = f32[5,2,24,128]{3,2,1,0:T(8,128)S(1)} collective-permute-done((f32[5,2,24,128]{3,2,1,0:T(8,128)S(1)}, f32[5,2,24,128]{3,2,1,0:T(8,128)S(1)}, u32[]{:S(2)}, u32[]{:S(2)}) %collective-permute-start.9) | collective-permute-done | bytes 122912 | tf_op jit(solution)/shard_map/ppermute | solution.py:443
  36.8 2.1 %collective-permute-done.10.refs_6_ = f32[5,2,40,128]{3,2,1,0:T(8,128)S(1)} collective-permute-done((f32[5,2,40,128]{3,2,1,0:T(8,128)S(1)}, f32[5,2,40,128]{3,2,1,0:T(8,128)S(1)}, u32[]{:S(2)}, u32[]{:S(2)}) %collective-permute-start.10) | collective-permute-done | bytes 204832 | tf_op jit(solution)/shard_map/ppermute | solution.py:443
  39.3 0.9 %collective-permute-done.14.refs_3_ = f32[5,2,24,128]{3,2,1,0:T(8,128)S(1)} collective-permute-done((f32[5,2,24,128]{3,2,1,0:T(8,128)S(1)}, f32[5,2,24,128]{3,2,1,0:T(8,128)S(1)}, u32[]{:S(2)}, u32[]{:S(2)}) %collective-permute-start.14) | collective-permute-done | bytes 122912 | tf_op jit(solution)/shard_map/ppermute | solution.py:443
  40.2 0.8 %shard_map.128 = f32[5,2,64,128]{3,2,1,0:T(8,128)} custom-call(f32[5,2,40,128]{3,2,1,0:T(8,128)S(1)} %shard_map.125.refs_0_, f32[5,2,40,128]{3,2,1,0:T(8,128)S(1)} %collective-permute-done.12.refs_1_, f32[5,2,24,128]{3,2,1,0:T(8,128)S(1)} %shard_map.122.refs_0_.refs_2_, f32[5,2,24,128]{3,2,1,0:T(8,128)S(1)} %collective-permute-done.14.refs_3_), custom_call_target="tpu_custom_call" | custom-call | flops 800000000 | bytes 983040 | tf_op jit(solution)/shard_map/pallas_call | solution.py:407
  (46 shorter events, 5.1 us)
Async XLA Ops:
  0.0 0.8 %copy-start.7 = (f32[2,64,128]{2,1,0:T(8,128)S(1)}, f32[2,64,128]{2,1,0:T(8,128)}, u32[]{:S(2)}) copy-start(f32[2,64,128]{2,1,0:T(8,128)} %refs_4_.1) | copy-start | bytes 196612
  0.0 0.9 %copy-start.6 = (f32[2,64,128]{2,1,0:T(8,128)S(1)}, f32[2,64,128]{2,1,0:T(8,128)}, u32[]{:S(2)}) copy-start(f32[2,64,128]{2,1,0:T(8,128)} %refs_3_.1) | copy-start | bytes 196612
  0.0 0.9 %copy-start.5 = (f32[2,64,128]{2,1,0:T(8,128)S(1)}, f32[2,64,128]{2,1,0:T(8,128)}, u32[]{:S(2)}) copy-start(f32[2,64,128]{2,1,0:T(8,128)} %refs_2_.1) | copy-start | bytes 196612
  0.0 0.9 %copy-start.4 = (f32[2,64,128]{2,1,0:T(8,128)S(1)}, f32[2,64,128]{2,1,0:T(8,128)}, u32[]{:S(2)}) copy-start(f32[2,64,128]{2,1,0:T(8,128)} %refs_1_.1) | copy-start | bytes 196612
  0.0 1.0 %copy-start.3 = (f32[2,64,128]{2,1,0:T(8,128)S(1)}, f32[2,64,128]{2,1,0:T(8,128)}, u32[]{:S(2)}) copy-start(f32[2,64,128]{2,1,0:T(8,128)} %refs_0_.1) | copy-start | bytes 196612
  0.0 4.9 %copy-start.1 = (f32[1,4,2,256,128]{4,3,2,1,0:T(8,128)S(1)}, f32[1,4,2,256,128]{4,3,2,1,0:T(8,128)}, u32[]{:S(2)}) copy-start(f32[1,4,2,256,128]{4,3,2,1,0:T(8,128)} %param.16) | copy-start | bytes 3145732
  1.0 4.0 %copy-start = (f32[1,4,2,256,128]{4,3,2,1,0:T(8,128)S(1)}, f32[1,4,2,256,128]{4,3,2,1,0:T(8,128)}, u32[]{:S(2)}) copy-start(f32[1,4,2,256,128]{4,3,2,1,0:T(8,128)} %param.17) | copy-start | bytes 3145732
  1.0 10.2 %copy-start.8 = (f32[1,2,256]{2,1,0:T(2,128)S(1)}, f32[1,2,256]{2,1,0:T(2,128)}, u32[]{:S(2)}) copy-start(f32[1,2,256]{2,1,0:T(2,128)} %param.21) | copy-start | bytes 6148
  1.0 10.2 %copy-start.9 = (s32[1,256]{1,0:T(1,128)S(1)}, s32[1,256]{1,0:T(1,128)}, u32[]{:S(2)}) copy-start(s32[1,256]{1,0:T(1,128)} %receivers.1) | copy-start | bytes 3076
  1.0 12.1 %collective-permute-start.2 = (f32[5,2,64,128]{3,2,1,0:T(8,128)S(1)}, f32[5,2,64,128]{3,2,1,0:T(8,128)S(1)}, u32[]{:S(2)}, u32[]{:S(2)}) collective-permute-start(f32[5,2,64,128]{3,2,1,0:T(8,128)S(1)} %shard_map.110.refs_0_.order), channel_id=1, source_target_pairs={{0,24},{8,16},{16,8},{24,0},{1,25},{9,17},{17,9},{25,1},{2,26},{10... | collective-permute-start | bytes 983048 | tf_op jit(solution)/shard_map/ppermute | solution.py:443
  5.0 8.3 %collective-permute-start.3 = (f32[4,256,128]{2,1,0:T(8,128)S(1)}, f32[4,256,128]{2,1,0:T(8,128)S(1)}, u32[]{:S(2)}, u32[]{:S(2)}) collective-permute-start(f32[4,256,128]{2,1,0:T(8,128)S(1)} %get-tuple-element.26), channel_id=1, source_target_pairs={{1,2},{3,4},{5,6},{2,1},{4,3},{6,5},{9,10},{11,12},{13,14},{10,9},... | collective-permute-start | bytes 1572872 | tf_op jit(solution)/shard_map/ppermute | solution.py:447
  5.7 7.6 %collective-permute-start.4 = (f32[4,256,128]{2,1,0:T(8,128)S(1)}, f32[4,256,128]{2,1,0:T(8,128)S(1)}, u32[]{:S(2)}, u32[]{:S(2)}) collective-permute-start(f32[4,256,128]{2,1,0:T(8,128)S(1)} %get-tuple-element.27), channel_id=1, source_target_pairs={{0,1},{2,3},{4,5},{6,7},{1,0},{3,2},{5,4},{7,6},{8,9},{10,11},{12,... | collective-permute-start | bytes 1572872 | tf_op jit(solution)/shard_map/ppermute | solution.py:447
  8.7 11.4 %collective-permute-start.1 = (f32[5,2,64,128]{3,2,1,0:T(8,128)S(1)}, f32[5,2,64,128]{3,2,1,0:T(8,128)S(1)}, u32[]{:S(2)}, u32[]{:S(2)}) collective-permute-start(f32[5,2,64,128]{3,2,1,0:T(8,128)S(1)} %shard_map.110.refs_0_.order), channel_id=1, source_target_pairs={{0,16},{8,24},{16,0},{24,8},{1,17},{9,25},{17,1},{25,9},{2,18},{10... | collective-permute-start | bytes 983048 | tf_op jit(solution)/shard_map/ppermute | solution.py:443
  9.2 10.9 %collective-permute-start = (f32[5,2,64,128]{3,2,1,0:T(8,128)S(1)}, f32[5,2,64,128]{3,2,1,0:T(8,128)S(1)}, u32[]{:S(2)}, u32[]{:S(2)}) collective-permute-start(f32[5,2,64,128]{3,2,1,0:T(8,128)S(1)} %shard_map.110.refs_0_.order), channel_id=1, source_target_pairs={{0,8},{8,0},{16,24},{24,16},{1,9},{9,1},{17,25},{25,17},{2,10},{10... | collective-permute-start | bytes 983048 | tf_op jit(solution)/shard_map/ppermute | solution.py:443
  14.7 10.1 %collective-permute-start.5 = (f32[2,128,128]{2,1,0:T(8,128)S(1)}, f32[2,128,128]{2,1,0:T(8,128)S(1)}, u32[]{:S(2)}, u32[]{:S(2)}) collective-permute-start(f32[2,128,128]{2,1,0:T(8,128)S(1)} %get-tuple-element.32), channel_id=1, source_target_pairs={{1,2},{3,4},{5,6},{2,1},{4,3},{6,5},{9,10},{11,12},{13,14},{10,9},... | collective-permute-start | bytes 393224 | tf_op jit(solution)/shard_map/ppermute | solution.py:447
  15.3 9.5 %collective-permute-start.6 = (f32[2,128,128]{2,1,0:T(8,128)S(1)}, f32[2,128,128]{2,1,0:T(8,128)S(1)}, u32[]{:S(2)}, u32[]{:S(2)}) collective-permute-start(f32[2,128,128]{2,1,0:T(8,128)S(1)} %get-tuple-element.33), channel_id=1, source_target_pairs={{0,1},{2,3},{4,5},{6,7},{1,0},{3,2},{5,4},{7,6},{8,9},{10,11},{12,... | collective-permute-start | bytes 393224 | tf_op jit(solution)/shard_map/ppermute | solution.py:447
  21.1 6.6 %collective-permute-start.7 = (f32[2,128,128]{2,1,0:T(8,128)S(1)}, f32[2,128,128]{2,1,0:T(8,128)S(1)}, u32[]{:S(2)}, u32[]{:S(2)}) collective-permute-start(f32[2,128,128]{2,1,0:T(8,128)S(1)} %get-tuple-element.34), channel_id=1, source_target_pairs={{1,2},{3,4},{5,6},{2,1},{4,3},{6,5},{9,10},{11,12},{13,14},{10,9},... | collective-permute-start | bytes 393224 | tf_op jit(solution)/shard_map/ppermute | solution.py:447
  21.8 5.9 %collective-permute-start.8 = (f32[2,128,128]{2,1,0:T(8,128)S(1)}, f32[2,128,128]{2,1,0:T(8,128)S(1)}, u32[]{:S(2)}, u32[]{:S(2)}) collective-permute-start(f32[2,128,128]{2,1,0:T(8,128)S(1)} %get-tuple-element.35), channel_id=1, source_target_pairs={{0,1},{2,3},{4,5},{6,7},{1,0},{3,2},{5,4},{7,6},{8,9},{10,11},{12,... | collective-permute-start | bytes 393224 | tf_op jit(solution)/shard_map/ppermute | solution.py:447
  25.6 7.1 %collective-permute-start.11 = (f32[5,2,40,128]{3,2,1,0:T(8,128)S(1)}, f32[5,2,40,128]{3,2,1,0:T(8,128)S(1)}, u32[]{:S(2)}, u32[]{:S(2)}) collective-permute-start(f32[5,2,40,128]{3,2,1,0:T(8,128)S(1)} %shard_map.118.refs_0_.order), channel_id=1, source_target_pairs={{0,8},{8,0},{16,24},{24,16},{1,9},{9,1},{17,25},{25,17},{2,10},{10... | collective-permute-start | bytes 614408 | tf_op jit(solution)/shard_map/ppermute | solution.py:443
  28.0 6.1 %collective-permute-start.13 = (f32[5,2,24,128]{3,2,1,0:T(8,128)S(1)}, f32[5,2,24,128]{3,2,1,0:T(8,128)S(1)}, u32[]{:S(2)}, u32[]{:S(2)}) collective-permute-start(f32[5,2,24,128]{3,2,1,0:T(8,128)S(1)} %shard_map.119.refs_0_), channel_id=1, source_target_pairs={{0,16},{8,24},{16,0},{24,8},{1,17},{9,25},{17,1},{25,9},{2,18},{10... | collective-permute-start | bytes 368648 | tf_op jit(solution)/shard_map/ppermute | solution.py:443
  30.1 6.4 %collective-permute-start.9 = (f32[5,2,24,128]{3,2,1,0:T(8,128)S(1)}, f32[5,2,24,128]{3,2,1,0:T(8,128)S(1)}, u32[]{:S(2)}, u32[]{:S(2)}) collective-permute-start(f32[5,2,24,128]{3,2,1,0:T(8,128)S(1)} %get-tuple-element.41.refs_0_), channel_id=1, source_target_pairs={{0,16},{8,24},{16,0},{24,8},{1,17},{9,25},{17,1},{25,9},{2,18},{10... | collective-permute-start | bytes 368648 | tf_op jit(solution)/shard_map/ppermute | solution.py:443
  31.3 7.6 %collective-permute-start.10 = (f32[5,2,40,128]{3,2,1,0:T(8,128)S(1)}, f32[5,2,40,128]{3,2,1,0:T(8,128)S(1)}, u32[]{:S(2)}, u32[]{:S(2)}) collective-permute-start(f32[5,2,40,128]{3,2,1,0:T(8,128)S(1)} %get-tuple-element.42), channel_id=1, source_target_pairs={{0,8},{8,0},{16,24},{24,16},{1,9},{9,1},{17,25},{25,17},{2,10},{10... | collective-permute-start | bytes 614408 | tf_op jit(solution)/shard_map/ppermute | solution.py:443
  32.7 7.5 %collective-permute-start.12 = (f32[5,2,40,128]{3,2,1,0:T(8,128)S(1)}, f32[5,2,40,128]{3,2,1,0:T(8,128)S(1)}, u32[]{:S(2)}, u32[]{:S(2)}) collective-permute-start(f32[5,2,40,128]{3,2,1,0:T(8,128)S(1)} %shard_map.126.order), channel_id=1, source_target_pairs={{0,16},{8,24},{16,0},{24,8},{1,17},{9,25},{17,1},{25,9},{2,18},{10... | collective-permute-start | bytes 614408 | tf_op jit(solution)/shard_map/ppermute | solution.py:443
  34.1 6.1 %collective-permute-start.14 = (f32[5,2,24,128]{3,2,1,0:T(8,128)S(1)}, f32[5,2,24,128]{3,2,1,0:T(8,128)S(1)}, u32[]{:S(2)}, u32[]{:S(2)}) collective-permute-start(f32[5,2,24,128]{3,2,1,0:T(8,128)S(1)} %shard_map.127), channel_id=1, source_target_pairs={{0,8},{8,0},{16,24},{24,16},{1,9},{9,1},{17,25},{25,17},{2,10},{10... | collective-permute-start | bytes 368648 | tf_op jit(solution)/shard_map/ppermute | solution.py:443
  (1 other events, 0.7 us)

commit v3 on v2

--- a/solution.py
+++ b/solution.py
@@ -9,7 +9,7 @@
 from jax.sharding import PartitionSpec as P
 
 STEPS = 2
-ROWS = 32
+ROWS = 8
 PAD = 8
 VMEM_LIMIT = 32 * 1024 * 1024
 FLOPS_PER_MICRO = 10**9

time: 41.2 us -> 40.9 us (level)
  transfers between devices with their start and end apart: 15 -> 15, of which waited for: 5 -> 5; matrix products, arithmetic and copies ran while one was open for 0% -> 0% of each run, Pallas kernels for 17% -> 16%
where the time goes in v3:
time: 40.9 us; the launch traced here: 40.7 us
  starting transfers between devices  25.8 us (63%)
  Pallas kernels  7.43 us (18%)
  waiting for transfers between devices  5.56 us (14%)
  local copies, waits for them, and re-layouts  1 us (2%)
  between operations  0.86 us (2%)
    ppermute x9, starting transfers between devices, swap(): lax.ppermute(values, 'shot', [(index, index ^ member) for index in range(...  13 us
    ppermute x6, starting transfers between devices, pair(): lax.ppermute(values, 'domain', pairs + [(target, source) for source, targ...  12.8 us
    pallas_call x20, Pallas kernels, call(): pl.pallas_call(kernel, out_shape=outs, in_specs=[VMEM] * len(operands), o...  7.43 us
    ppermute x9, waiting for transfers between devices, swap(): lax.ppermute(values, 'shot', [(index, index ^ member) for index in range(...  5.54 us
    unnamed x20, local copies, waits for them, and re-layouts  1 us
  transfers between devices with their start and end apart: 15, of which 5 were waited for; matrix products, arithmetic and copies ran while one was open for 0% of the time, Pallas kernels for 16%

profile of v3, /device:TPU:0, one launch (start us, length us, event | category | flops | bytes accessed | tf_op | source)
XLA Modules:
  0.0 40.7 jit_solution(10307686635237495265)
XLA Ops:
  1.0 4.0 %collective-permute-start.2 = (f32[5,2,64,128]{3,2,1,0:T(8,128)S(1)}, f32[5,2,64,128]{3,2,1,0:T(8,128)S(1)}, u32[]{:S(2)}, u32[]{:S(2)}) collective-permute-start(f32[5,2,64,128]{3,2,1,0:T(8,128)S(1)} %shard_map.110.refs_0_.order), channel_id=1, source_target_pairs={{0,24},{8,16},{16,8},{24,0},{1,25},{9,17},{17,9},{25,1},{2,26},{10... | collective-permute-start | bytes 983048 | tf_op jit(solution)/shard_map/ppermute | solution.py:443
  5.0 0.7 %collective-permute-start.3 = (f32[4,256,128]{2,1,0:T(8,128)S(1)}, f32[4,256,128]{2,1,0:T(8,128)S(1)}, u32[]{:S(2)}, u32[]{:S(2)}) collective-permute-start(f32[4,256,128]{2,1,0:T(8,128)S(1)} %get-tuple-element.26), channel_id=1, source_target_pairs={{1,2},{3,4},{5,6},{2,1},{4,3},{6,5},{9,10},{11,12},{13,14},{10,9},... | collective-permute-start | bytes 1572872 | tf_op jit(solution)/shard_map/ppermute | solution.py:447
  5.7 3.0 %collective-permute-start.4 = (f32[4,256,128]{2,1,0:T(8,128)S(1)}, f32[4,256,128]{2,1,0:T(8,128)S(1)}, u32[]{:S(2)}, u32[]{:S(2)}) collective-permute-start(f32[4,256,128]{2,1,0:T(8,128)S(1)} %get-tuple-element.27), channel_id=1, source_target_pairs={{0,1},{2,3},{4,5},{6,7},{1,0},{3,2},{5,4},{7,6},{8,9},{10,11},{12,... | collective-permute-start | bytes 1572872 | tf_op jit(solution)/shard_map/ppermute | solution.py:447
  9.2 1.3 %collective-permute-start = (f32[5,2,64,128]{3,2,1,0:T(8,128)S(1)}, f32[5,2,64,128]{3,2,1,0:T(8,128)S(1)}, u32[]{:S(2)}, u32[]{:S(2)}) collective-permute-start(f32[5,2,64,128]{3,2,1,0:T(8,128)S(1)} %shard_map.110.refs_0_.order), channel_id=1, source_target_pairs={{0,8},{8,0},{16,24},{24,16},{1,9},{9,1},{17,25},{25,17},{2,10},{10... | collective-permute-start | bytes 983048 | tf_op jit(solution)/shard_map/ppermute | solution.py:443
  11.1 0.7 %shard_map.111 = (f32[2,256,128]{2,1,0:T(8,128)S(1)}, f32[2,256,128]{2,1,0:T(8,128)S(1)}) custom-call(s32[1,256]{1,0:T(1,128)S(1)} %copy-done.9, f32[2,256]{1,0:T(2,128)S(1)} %bitcast.32), custom_call_target="tpu_custom_call" | custom-call | flops 1500000000 | bytes 527360 | tf_op jit(solution)/shard_map/pallas_call | solution.py:407
  11.8 1.3 %collective-permute-done.2.refs_1_ = f32[5,2,64,128]{3,2,1,0:T(8,128)S(1)} collective-permute-done((f32[5,2,64,128]{3,2,1,0:T(8,128)S(1)}, f32[5,2,64,128]{3,2,1,0:T(8,128)S(1)}, u32[]{:S(2)}, u32[]{:S(2)}) %collective-permute-start.2) | collective-permute-done | bytes 327712 | tf_op jit(solution)/shard_map/ppermute | solution.py:443
  13.7 0.8 %shard_map.114 = (f32[2,2,256,128]{3,2,1,0:T(8,128)S(1)}, f32[6,2,256,128]{3,2,1,0:T(8,128)S(1)}, f32[2,128,128]{2,1,0:T(8,128)S(1)}, f32[2,128,128]{2,1,0:T(8,128)S(1)}, f32[2,4,272,128]{3,2,1,0:T(8,128)S(1)}) custom-call(s32[2,256,128]{2,1,0:T(8,128)S(1)} %shard_map.109.order.cells, s32[1,1]{1,0:T(1,128)} %bitcast.4.source, f32[1,2]{1,0:T(1,128)S(1)} %copy-done.2, ...), custom_call_target="tpu_custom_call" | custom-call | flops 1200000000 | bytes 7667724 | tf_op jit(solution)/shard_map/pallas_call | solution.py:407
  14.5 0.7 %collective-permute-start.5 = (f32[2,128,128]{2,1,0:T(8,128)S(1)}, f32[2,128,128]{2,1,0:T(8,128)S(1)}, u32[]{:S(2)}, u32[]{:S(2)}) collective-permute-start(f32[2,128,128]{2,1,0:T(8,128)S(1)} %get-tuple-element.32), channel_id=1, source_target_pairs={{1,2},{3,4},{5,6},{2,1},{4,3},{6,5},{9,10},{11,12},{13,14},{10,9},... | collective-permute-start | bytes 393224 | tf_op jit(solution)/shard_map/ppermute | solution.py:447
  15.2 4.8 %collective-permute-start.6 = (f32[2,128,128]{2,1,0:T(8,128)S(1)}, f32[2,128,128]{2,1,0:T(8,128)S(1)}, u32[]{:S(2)}, u32[]{:S(2)}) collective-permute-start(f32[2,128,128]{2,1,0:T(8,128)S(1)} %get-tuple-element.33), channel_id=1, source_target_pairs={{0,1},{2,3},{4,5},{6,7},{1,0},{3,2},{5,4},{7,6},{8,9},{10,11},{12,... | collective-permute-start | bytes 393224 | tf_op jit(solution)/shard_map/ppermute | solution.py:447
  20.0 0.9 %shard_map.115 = (f32[7,2,256,128]{3,2,1,0:T(8,128)S(1)}, f32[2,2,256,128]{3,2,1,0:T(8,128)S(1)}, f32[6,2,256,128]{3,2,1,0:T(8,128)S(1)}, f32[2,128,128]{2,1,0:T(8,128)S(1)}, f32[2,128,128]{2,1,0:T(8,128)S(1)}) custom-call(s32[2,256,128]{2,1,0:T(8,128)S(1)} %shard_map.109.order.cells, ...), custom_call_target="tpu_custom_call", output_to_operand_aliasing={{0}: (7, {}), {1}: (8, {}), {2}: (9, {})} | custom-call | flops 1200000000 | bytes 11206668 | tf_op jit(solution)/shard_map/pallas_call | solution.py:407
  21.0 0.7 %collective-permute-start.7 = (f32[2,128,128]{2,1,0:T(8,128)S(1)}, f32[2,128,128]{2,1,0:T(8,128)S(1)}, u32[]{:S(2)}, u32[]{:S(2)}) collective-permute-start(f32[2,128,128]{2,1,0:T(8,128)S(1)} %get-tuple-element.34), channel_id=1, source_target_pairs={{1,2},{3,4},{5,6},{2,1},{4,3},{6,5},{9,10},{11,12},{13,14},{10,9},... | collective-permute-start | bytes 393224 | tf_op jit(solution)/shard_map/ppermute | solution.py:447
  21.6 3.0 %collective-permute-start.8 = (f32[2,128,128]{2,1,0:T(8,128)S(1)}, f32[2,128,128]{2,1,0:T(8,128)S(1)}, u32[]{:S(2)}, u32[]{:S(2)}) collective-permute-start(f32[2,128,128]{2,1,0:T(8,128)S(1)} %get-tuple-element.35), channel_id=1, source_target_pairs={{0,1},{2,3},{4,5},{6,7},{1,0},{3,2},{5,4},{7,6},{8,9},{10,11},{12,... | collective-permute-start | bytes 393224 | tf_op jit(solution)/shard_map/ppermute | solution.py:447
  25.4 1.5 %collective-permute-start.11 = (f32[5,2,40,128]{3,2,1,0:T(8,128)S(1)}, f32[5,2,40,128]{3,2,1,0:T(8,128)S(1)}, u32[]{:S(2)}, u32[]{:S(2)}) collective-permute-start(f32[5,2,40,128]{3,2,1,0:T(8,128)S(1)} %shard_map.118.refs_0_.order), channel_id=1, source_target_pairs={{0,8},{8,0},{16,24},{24,16},{1,9},{9,1},{17,25},{25,17},{2,10},{10... | collective-permute-start | bytes 614408 | tf_op jit(solution)/shard_map/ppermute | solution.py:443
  27.7 1.5 %collective-permute-start.13 = (f32[5,2,24,128]{3,2,1,0:T(8,128)S(1)}, f32[5,2,24,128]{3,2,1,0:T(8,128)S(1)}, u32[]{:S(2)}, u32[]{:S(2)}) collective-permute-start(f32[5,2,24,128]{3,2,1,0:T(8,128)S(1)} %shard_map.119.refs_0_), channel_id=1, source_target_pairs={{0,16},{8,24},{16,0},{24,8},{1,17},{9,25},{17,1},{25,9},{2,18},{10... | collective-permute-start | bytes 368648 | tf_op jit(solution)/shard_map/ppermute | solution.py:443
  29.3 0.5 %shard_map.121 = (f32[5,2,40,128]{3,2,1,0:T(8,128)S(1)}, f32[5,2,24,128]{3,2,1,0:T(8,128)S(1)}) custom-call(s32[2,256,128]{2,1,0:T(8,128)S(1)} %shard_map.109.order.cells, s32[1,1]{1,0:T(1,128)} %bitcast.8.source, f32[1,2]{1,0:T(1,128)S(1)} %copy-done.2, f32[4,2,256,128]{3,2,1,0:T(8,128)S(1)} %bitcast.28, f32[4,2,256,128]{3,2,1,0:T(8,128)S(1)} %bitcast.18, ...), custom_call_target="tpu_custom_call" | custom-call | flops 1200000000 | bytes 7921676 | tf_op jit(solution)/shard_map/pallas_call | solution.py:407
  29.8 0.6 %collective-permute-start.9 = (f32[5,2,24,128]{3,2,1,0:T(8,128)S(1)}, f32[5,2,24,128]{3,2,1,0:T(8,128)S(1)}, u32[]{:S(2)}, u32[]{:S(2)}) collective-permute-start(f32[5,2,24,128]{3,2,1,0:T(8,128)S(1)} %get-tuple-element.41.refs_0_), channel_id=1, source_target_pairs={{0,16},{8,24},{16,0},{24,8},{1,17},{9,25},{17,1},{25,9},{2,18},{10... | collective-permute-start | bytes 368648 | tf_op jit(solution)/shard_map/ppermute | solution.py:443
  30.5 0.5 %shard_map.124 = (f32[5,2,40,128]{3,2,1,0:T(8,128)S(1)}, f32[5,2,24,128]{3,2,1,0:T(8,128)S(1)}) custom-call(s32[2,256,128]{2,1,0:T(8,128)S(1)} %shard_map.109.order.cells, s32[1,1]{1,0:T(1,128)} %bitcast.10.source, f32[1,2]{1,0:T(1,128)S(1)} %copy-done.2, f32[4,2,256,128]{3,2,1,0:T(8,128)S(1)} %bitcast.29, f32[4,2,256,128]{3,2,1,0:T(8,128)S(1)} %bitcast.19, ...), custom_call_target="tpu_custom_call" | custom-call | flops 1200000000 | bytes 7921676 | tf_op jit(solution)/shard_map/pallas_call | solution.py:407
  31.0 0.7 %collective-permute-start.10 = (f32[5,2,40,128]{3,2,1,0:T(8,128)S(1)}, f32[5,2,40,128]{3,2,1,0:T(8,128)S(1)}, u32[]{:S(2)}, u32[]{:S(2)}) collective-permute-start(f32[5,2,40,128]{3,2,1,0:T(8,128)S(1)} %get-tuple-element.42), channel_id=1, source_target_pairs={{0,8},{8,0},{16,24},{24,16},{1,9},{9,1},{17,25},{25,17},{2,10},{10... | collective-permute-start | bytes 614408 | tf_op jit(solution)/shard_map/ppermute | solution.py:443
  32.5 1.4 %collective-permute-start.12 = (f32[5,2,40,128]{3,2,1,0:T(8,128)S(1)}, f32[5,2,40,128]{3,2,1,0:T(8,128)S(1)}, u32[]{:S(2)}, u32[]{:S(2)}) collective-permute-start(f32[5,2,40,128]{3,2,1,0:T(8,128)S(1)} %shard_map.126.order), channel_id=1, source_target_pairs={{0,16},{8,24},{16,0},{24,8},{1,17},{9,25},{17,1},{25,9},{2,18},{10... | collective-permute-start | bytes 614408 | tf_op jit(solution)/shard_map/ppermute | solution.py:443
  33.9 1.6 %collective-permute-start.14 = (f32[5,2,24,128]{3,2,1,0:T(8,128)S(1)}, f32[5,2,24,128]{3,2,1,0:T(8,128)S(1)}, u32[]{:S(2)}, u32[]{:S(2)}) collective-permute-start(f32[5,2,24,128]{3,2,1,0:T(8,128)S(1)} %shard_map.127), channel_id=1, source_target_pairs={{0,8},{8,0},{16,24},{24,16},{1,9},{9,1},{17,25},{25,17},{2,10},{10... | collective-permute-start | bytes 368648 | tf_op jit(solution)/shard_map/ppermute | solution.py:443
  35.5 0.9 %collective-permute-done.9.refs_7_ = f32[5,2,24,128]{3,2,1,0:T(8,128)S(1)} collective-permute-done((f32[5,2,24,128]{3,2,1,0:T(8,128)S(1)}, f32[5,2,24,128]{3,2,1,0:T(8,128)S(1)}, u32[]{:S(2)}, u32[]{:S(2)}) %collective-permute-start.9) | collective-permute-done | bytes 122912 | tf_op jit(solution)/shard_map/ppermute | solution.py:443
  36.6 2.0 %collective-permute-done.10.refs_6_ = f32[5,2,40,128]{3,2,1,0:T(8,128)S(1)} collective-permute-done((f32[5,2,40,128]{3,2,1,0:T(8,128)S(1)}, f32[5,2,40,128]{3,2,1,0:T(8,128)S(1)}, u32[]{:S(2)}, u32[]{:S(2)}) %collective-permute-start.10) | collective-permute-done | bytes 204832 | tf_op jit(solution)/shard_map/ppermute | solution.py:443
  39.0 1.0 %collective-permute-done.14.refs_3_ = f32[5,2,24,128]{3,2,1,0:T(8,128)S(1)} collective-permute-done((f32[5,2,24,128]{3,2,1,0:T(8,128)S(1)}, f32[5,2,24,128]{3,2,1,0:T(8,128)S(1)}, u32[]{:S(2)}, u32[]{:S(2)}) %collective-permute-start.14) | collective-permute-done | bytes 122912 | tf_op jit(solution)/shard_map/ppermute | solution.py:443
  39.9 0.8 %shard_map.128 = f32[5,2,64,128]{3,2,1,0:T(8,128)} custom-call(f32[5,2,40,128]{3,2,1,0:T(8,128)S(1)} %shard_map.125.refs_0_, f32[5,2,40,128]{3,2,1,0:T(8,128)S(1)} %collective-permute-done.12.refs_1_, f32[5,2,24,128]{3,2,1,0:T(8,128)S(1)} %shard_map.122.refs_0_.refs_2_, f32[5,2,24,128]{3,2,1,0:T(8,128)S(1)} %collective-permute-done.14.refs_3_), custom_call_target="tpu_custom_call" | custom-call | flops 800000000 | bytes 983040 | tf_op jit(solution)/shard_map/pallas_call | solution.py:407
  (46 shorter events, 5.2 us)
Async XLA Ops:
  0.0 0.8 %copy-start.7 = (f32[2,64,128]{2,1,0:T(8,128)S(1)}, f32[2,64,128]{2,1,0:T(8,128)}, u32[]{:S(2)}) copy-start(f32[2,64,128]{2,1,0:T(8,128)} %refs_4_.1) | copy-start | bytes 196612
  0.0 0.9 %copy-start.6 = (f32[2,64,128]{2,1,0:T(8,128)S(1)}, f32[2,64,128]{2,1,0:T(8,128)}, u32[]{:S(2)}) copy-start(f32[2,64,128]{2,1,0:T(8,128)} %refs_3_.1) | copy-start | bytes 196612
  0.0 0.9 %copy-start.5 = (f32[2,64,128]{2,1,0:T(8,128)S(1)}, f32[2,64,128]{2,1,0:T(8,128)}, u32[]{:S(2)}) copy-start(f32[2,64,128]{2,1,0:T(8,128)} %refs_2_.1) | copy-start | bytes 196612
  0.0 0.9 %copy-start.4 = (f32[2,64,128]{2,1,0:T(8,128)S(1)}, f32[2,64,128]{2,1,0:T(8,128)}, u32[]{:S(2)}) copy-start(f32[2,64,128]{2,1,0:T(8,128)} %refs_1_.1) | copy-start | bytes 196612
  0.0 1.0 %copy-start.3 = (f32[2,64,128]{2,1,0:T(8,128)S(1)}, f32[2,64,128]{2,1,0:T(8,128)}, u32[]{:S(2)}) copy-start(f32[2,64,128]{2,1,0:T(8,128)} %refs_0_.1) | copy-start | bytes 196612
  0.0 4.9 %copy-start.1 = (f32[1,4,2,256,128]{4,3,2,1,0:T(8,128)S(1)}, f32[1,4,2,256,128]{4,3,2,1,0:T(8,128)}, u32[]{:S(2)}) copy-start(f32[1,4,2,256,128]{4,3,2,1,0:T(8,128)} %param.16) | copy-start | bytes 3145732
  1.0 4.0 %copy-start = (f32[1,4,2,256,128]{4,3,2,1,0:T(8,128)S(1)}, f32[1,4,2,256,128]{4,3,2,1,0:T(8,128)}, u32[]{:S(2)}) copy-start(f32[1,4,2,256,128]{4,3,2,1,0:T(8,128)} %param.17) | copy-start | bytes 3145732
  1.0 10.2 %copy-start.8 = (f32[1,2,256]{2,1,0:T(2,128)S(1)}, f32[1,2,256]{2,1,0:T(2,128)}, u32[]{:S(2)}) copy-start(f32[1,2,256]{2,1,0:T(2,128)} %param.21) | copy-start | bytes 6148
  1.0 10.2 %copy-start.9 = (s32[1,256]{1,0:T(1,128)S(1)}, s32[1,256]{1,0:T(1,128)}, u32[]{:S(2)}) copy-start(s32[1,256]{1,0:T(1,128)} %receivers.1) | copy-start | bytes 3076
  1.0 12.1 %collective-permute-start.2 = (f32[5,2,64,128]{3,2,1,0:T(8,128)S(1)}, f32[5,2,64,128]{3,2,1,0:T(8,128)S(1)}, u32[]{:S(2)}, u32[]{:S(2)}) collective-permute-start(f32[5,2,64,128]{3,2,1,0:T(8,128)S(1)} %shard_map.110.refs_0_.order), channel_id=1, source_target_pairs={{0,24},{8,16},{16,8},{24,0},{1,25},{9,17},{17,9},{25,1},{2,26},{10... | collective-permute-start | bytes 983048 | tf_op jit(solution)/shard_map/ppermute | solution.py:443
  5.0 8.3 %collective-permute-start.3 = (f32[4,256,128]{2,1,0:T(8,128)S(1)}, f32[4,256,128]{2,1,0:T(8,128)S(1)}, u32[]{:S(2)}, u32[]{:S(2)}) collective-permute-start(f32[4,256,128]{2,1,0:T(8,128)S(1)} %get-tuple-element.26), channel_id=1, source_target_pairs={{1,2},{3,4},{5,6},{2,1},{4,3},{6,5},{9,10},{11,12},{13,14},{10,9},... | collective-permute-start | bytes 1572872 | tf_op jit(solution)/shard_map/ppermute | solution.py:447
  5.7 7.6 %collective-permute-start.4 = (f32[4,256,128]{2,1,0:T(8,128)S(1)}, f32[4,256,128]{2,1,0:T(8,128)S(1)}, u32[]{:S(2)}, u32[]{:S(2)}) collective-permute-start(f32[4,256,128]{2,1,0:T(8,128)S(1)} %get-tuple-element.27), channel_id=1, source_target_pairs={{0,1},{2,3},{4,5},{6,7},{1,0},{3,2},{5,4},{7,6},{8,9},{10,11},{12,... | collective-permute-start | bytes 1572872 | tf_op jit(solution)/shard_map/ppermute | solution.py:447
  8.7 11.3 %collective-permute-start.1 = (f32[5,2,64,128]{3,2,1,0:T(8,128)S(1)}, f32[5,2,64,128]{3,2,1,0:T(8,128)S(1)}, u32[]{:S(2)}, u32[]{:S(2)}) collective-permute-start(f32[5,2,64,128]{3,2,1,0:T(8,128)S(1)} %shard_map.110.refs_0_.order), channel_id=1, source_target_pairs={{0,16},{8,24},{16,0},{24,8},{1,17},{9,25},{17,1},{25,9},{2,18},{10... | collective-permute-start | bytes 983048 | tf_op jit(solution)/shard_map/ppermute | solution.py:443
  9.2 10.8 %collective-permute-start = (f32[5,2,64,128]{3,2,1,0:T(8,128)S(1)}, f32[5,2,64,128]{3,2,1,0:T(8,128)S(1)}, u32[]{:S(2)}, u32[]{:S(2)}) collective-permute-start(f32[5,2,64,128]{3,2,1,0:T(8,128)S(1)} %shard_map.110.refs_0_.order), channel_id=1, source_target_pairs={{0,8},{8,0},{16,24},{24,16},{1,9},{9,1},{17,25},{25,17},{2,10},{10... | collective-permute-start | bytes 983048 | tf_op jit(solution)/shard_map/ppermute | solution.py:443
  14.5 10.1 %collective-permute-start.5 = (f32[2,128,128]{2,1,0:T(8,128)S(1)}, f32[2,128,128]{2,1,0:T(8,128)S(1)}, u32[]{:S(2)}, u32[]{:S(2)}) collective-permute-start(f32[2,128,128]{2,1,0:T(8,128)S(1)} %get-tuple-element.32), channel_id=1, source_target_pairs={{1,2},{3,4},{5,6},{2,1},{4,3},{6,5},{9,10},{11,12},{13,14},{10,9},... | collective-permute-start | bytes 393224 | tf_op jit(solution)/shard_map/ppermute | solution.py:447
  15.2 9.4 %collective-permute-start.6 = (f32[2,128,128]{2,1,0:T(8,128)S(1)}, f32[2,128,128]{2,1,0:T(8,128)S(1)}, u32[]{:S(2)}, u32[]{:S(2)}) collective-permute-start(f32[2,128,128]{2,1,0:T(8,128)S(1)} %get-tuple-element.33), channel_id=1, source_target_pairs={{0,1},{2,3},{4,5},{6,7},{1,0},{3,2},{5,4},{7,6},{8,9},{10,11},{12,... | collective-permute-start | bytes 393224 | tf_op jit(solution)/shard_map/ppermute | solution.py:447
  21.0 6.5 %collective-permute-start.7 = (f32[2,128,128]{2,1,0:T(8,128)S(1)}, f32[2,128,128]{2,1,0:T(8,128)S(1)}, u32[]{:S(2)}, u32[]{:S(2)}) collective-permute-start(f32[2,128,128]{2,1,0:T(8,128)S(1)} %get-tuple-element.34), channel_id=1, source_target_pairs={{1,2},{3,4},{5,6},{2,1},{4,3},{6,5},{9,10},{11,12},{13,14},{10,9},... | collective-permute-start | bytes 393224 | tf_op jit(solution)/shard_map/ppermute | solution.py:447
  21.6 5.8 %collective-permute-start.8 = (f32[2,128,128]{2,1,0:T(8,128)S(1)}, f32[2,128,128]{2,1,0:T(8,128)S(1)}, u32[]{:S(2)}, u32[]{:S(2)}) collective-permute-start(f32[2,128,128]{2,1,0:T(8,128)S(1)} %get-tuple-element.35), channel_id=1, source_target_pairs={{0,1},{2,3},{4,5},{6,7},{1,0},{3,2},{5,4},{7,6},{8,9},{10,11},{12,... | collective-permute-start | bytes 393224 | tf_op jit(solution)/shard_map/ppermute | solution.py:447
  25.4 7.1 %collective-permute-start.11 = (f32[5,2,40,128]{3,2,1,0:T(8,128)S(1)}, f32[5,2,40,128]{3,2,1,0:T(8,128)S(1)}, u32[]{:S(2)}, u32[]{:S(2)}) collective-permute-start(f32[5,2,40,128]{3,2,1,0:T(8,128)S(1)} %shard_map.118.refs_0_.order), channel_id=1, source_target_pairs={{0,8},{8,0},{16,24},{24,16},{1,9},{9,1},{17,25},{25,17},{2,10},{10... | collective-permute-start | bytes 614408 | tf_op jit(solution)/shard_map/ppermute | solution.py:443
  27.7 6.2 %collective-permute-start.13 = (f32[5,2,24,128]{3,2,1,0:T(8,128)S(1)}, f32[5,2,24,128]{3,2,1,0:T(8,128)S(1)}, u32[]{:S(2)}, u32[]{:S(2)}) collective-permute-start(f32[5,2,24,128]{3,2,1,0:T(8,128)S(1)} %shard_map.119.refs_0_), channel_id=1, source_target_pairs={{0,16},{8,24},{16,0},{24,8},{1,17},{9,25},{17,1},{25,9},{2,18},{10... | collective-permute-start | bytes 368648 | tf_op jit(solution)/shard_map/ppermute | solution.py:443
  29.8 6.6 %collective-permute-start.9 = (f32[5,2,24,128]{3,2,1,0:T(8,128)S(1)}, f32[5,2,24,128]{3,2,1,0:T(8,128)S(1)}, u32[]{:S(2)}, u32[]{:S(2)}) collective-permute-start(f32[5,2,24,128]{3,2,1,0:T(8,128)S(1)} %get-tuple-element.41.refs_0_), channel_id=1, source_target_pairs={{0,16},{8,24},{16,0},{24,8},{1,17},{9,25},{17,1},{25,9},{2,18},{10... | collective-permute-start | bytes 368648 | tf_op jit(solution)/shard_map/ppermute | solution.py:443
  31.0 7.6 %collective-permute-start.10 = (f32[5,2,40,128]{3,2,1,0:T(8,128)S(1)}, f32[5,2,40,128]{3,2,1,0:T(8,128)S(1)}, u32[]{:S(2)}, u32[]{:S(2)}) collective-permute-start(f32[5,2,40,128]{3,2,1,0:T(8,128)S(1)} %get-tuple-element.42), channel_id=1, source_target_pairs={{0,8},{8,0},{16,24},{24,16},{1,9},{9,1},{17,25},{25,17},{2,10},{10... | collective-permute-start | bytes 614408 | tf_op jit(solution)/shard_map/ppermute | solution.py:443
  32.5 7.4 %collective-permute-start.12 = (f32[5,2,40,128]{3,2,1,0:T(8,128)S(1)}, f32[5,2,40,128]{3,2,1,0:T(8,128)S(1)}, u32[]{:S(2)}, u32[]{:S(2)}) collective-permute-start(f32[5,2,40,128]{3,2,1,0:T(8,128)S(1)} %shard_map.126.order), channel_id=1, source_target_pairs={{0,16},{8,24},{16,0},{24,8},{1,17},{9,25},{17,1},{25,9},{2,18},{10... | collective-permute-start | bytes 614408 | tf_op jit(solution)/shard_map/ppermute | solution.py:443
  33.9 6.0 %collective-permute-start.14 = (f32[5,2,24,128]{3,2,1,0:T(8,128)S(1)}, f32[5,2,24,128]{3,2,1,0:T(8,128)S(1)}, u32[]{:S(2)}, u32[]{:S(2)}) collective-permute-start(f32[5,2,24,128]{3,2,1,0:T(8,128)S(1)} %shard_map.127), channel_id=1, source_target_pairs={{0,8},{8,0},{16,24},{24,16},{1,9},{9,1},{17,25},{25,17},{2,10},{10... | collective-permute-start | bytes 368648 | tf_op jit(solution)/shard_map/ppermute | solution.py:443
  (1 other events, 0.7 us)

commit v4 on v0

--- a/solution.py
+++ b/solution.py
@@ -302,7 +302,8 @@
                  *refs):
     sided = 1 in parts
     refs = list(refs)[1 if ordered else 0 :]
-    outer_rest, inner_rest = (refs.pop(0), refs.pop(0)) if sided else (None, None)
+    with_rest = sided or 0 < member < shots - 1
+    outer_rest, inner_rest = (refs.pop(0), refs.pop(0)) if with_rest else (None, None)
     table, terms, late, hits, sums, *refs = refs
     padded = refs.pop()
     came, results = refs[: -len(parts)], refs[-len(parts) :]
@@ -502,12 +503,16 @@
             functools.partial(backward_kernel, shots, member, False), [late_shape], 0.6, after, ring, table
         )[0]
 
+    late = {}
+
     def image(member, parts=(0, 1), came=(), order=()):
-        rest_edges = (outer_rest, inner_rest) if 1 in parts else ()
+        rest_edges = (outer_rest, inner_rest) if 1 in parts or 0 < member < last else ()
+        if member not in late:
+            late[member] = late_of(member)
         return call(
             functools.partial(image_kernel, shots, member, cut, parts, bool(order)), [piece_shapes[part] for part in parts], 1.2,
             cells, spot, wave, before, after, fields, outer_near, inner_near, *order, *rest_edges,
-            table, terms, late_of(member), hits, sums, *came,
+            table, terms, late[member], hits, sums, *came,
             scratch=[pltpu.VMEM((2, depth + 2, quarter + 2 * PAD, length), jnp.float32)],
         )
 
@@ -516,10 +521,12 @@
         from_x = swap(far_first, 1)
         (far_second,) = image(3, (1,), order=(far_first,))
         from_y = swap(far_second, 2)
-        y_first, y_second = image(2, order=(far_second,))
+        (y_second,) = image(2, (1,), order=(far_second,))
         near_y = swap(y_second, 2)
-        x_first, x_second = image(1, order=(y_second,))
+        (x_first,) = image(1, (0,), order=(y_second,))
         near_x = swap(x_first, 1)
+        (y_first,) = image(2, (0,), order=(x_first,))
+        (x_second,) = image(1, (1,), order=(y_first,))
         (y_first,) = call(add_kernel, piece_shapes[:1], 0.1, y_first, from_x, far_first)
         over_y = swap(y_first, 2)
         (x_second,) = call(add_kernel, piece_shapes[1:], 0.1, x_second, from_y, y_first)

time: 41 us -> 40.9 us (level)
    pallas_call x20 -> x22, Pallas kernels: 7.47 us -> 7.65 us  [call(): pl.pallas_call(kernel, out_shape=outs, in_specs=[VMEM] * len(operands), o...]
  transfers between devices with their start and end apart: 15 -> 15, of which waited for: 5 -> 7; matrix products, arithmetic and copies ran while one was open for 0% -> 0% of each run, Pallas kernels for 16% -> 16%
where the time goes in v4:
time: 40.9 us; the launch traced here: 40.7 us
  starting transfers between devices  25.7 us (63%)
  Pallas kernels  7.65 us (19%)
  waiting for transfers between devices  5.36 us (13%)
  local copies, waits for them, and re-layouts  1.14 us (3%)
  between operations  0.88 us (2%)
    ppermute x9, starting transfers between devices, swap(): lax.ppermute(values, 'shot', [(index, index ^ member) for index in range(...  12.9 us
    ppermute x6, starting transfers between devices, pair(): lax.ppermute(values, 'domain', pairs + [(target, source) for source, targ...  12.8 us
    pallas_call x22, Pallas kernels, call(): pl.pallas_call(kernel, out_shape=outs, in_specs=[VMEM] * len(operands), o...  7.65 us
    ppermute x9, waiting for transfers between devices, swap(): lax.ppermute(values, 'shot', [(index, index ^ member) for index in range(...  5.35 us
    unnamed x20, local copies, waits for them, and re-layouts  1.14 us
  transfers between devices with their start and end apart: 15, of which 7 were waited for; matrix products, arithmetic and copies ran while one was open for 0% of the time, Pallas kernels for 16%

profile of v4, /device:TPU:0, one launch (start us, length us, event | category | flops | bytes accessed | tf_op | source)
XLA Modules:
  0.0 40.7 jit_solution(583381254581596654)
XLA Ops:
  0.2 0.6 %copy-done.7 = f32[2,64,128]{2,1,0:T(8,128)S(1)} copy-done((f32[2,64,128]{2,1,0:T(8,128)S(1)}, f32[2,64,128]{2,1,0:T(8,128)}, u32[]{:S(2)}) %copy-start.7) | copy-done | bytes 65560
  1.0 4.0 %collective-permute-start.2 = (f32[5,2,64,128]{3,2,1,0:T(8,128)S(1)}, f32[5,2,64,128]{3,2,1,0:T(8,128)S(1)}, u32[]{:S(2)}, u32[]{:S(2)}) collective-permute-start(f32[5,2,64,128]{3,2,1,0:T(8,128)S(1)} %shard_map.110.refs_0_.order), channel_id=1, source_target_pairs={{0,24},{8,16},{16,8},{24,0},{1,25},{9,17},{17,9},{25,1},{2,26},{10... | collective-permute-start | bytes 983048 | tf_op jit(solution)/shard_map/ppermute | solution.py:444
  5.0 0.7 %collective-permute-start.3 = (f32[4,256,128]{2,1,0:T(8,128)S(1)}, f32[4,256,128]{2,1,0:T(8,128)S(1)}, u32[]{:S(2)}, u32[]{:S(2)}) collective-permute-start(f32[4,256,128]{2,1,0:T(8,128)S(1)} %get-tuple-element.22), channel_id=1, source_target_pairs={{1,2},{3,4},{5,6},{2,1},{4,3},{6,5},{9,10},{11,12},{13,14},{10,9},... | collective-permute-start | bytes 1572872 | tf_op jit(solution)/shard_map/ppermute | solution.py:448
  5.7 3.0 %collective-permute-start.4 = (f32[4,256,128]{2,1,0:T(8,128)S(1)}, f32[4,256,128]{2,1,0:T(8,128)S(1)}, u32[]{:S(2)}, u32[]{:S(2)}) collective-permute-start(f32[4,256,128]{2,1,0:T(8,128)S(1)} %get-tuple-element.23), channel_id=1, source_target_pairs={{0,1},{2,3},{4,5},{6,7},{1,0},{3,2},{5,4},{7,6},{8,9},{10,11},{12,... | collective-permute-start | bytes 1572872 | tf_op jit(solution)/shard_map/ppermute | solution.py:448
  8.7 0.5 %collective-permute-start.1 = (f32[5,2,64,128]{3,2,1,0:T(8,128)S(1)}, f32[5,2,64,128]{3,2,1,0:T(8,128)S(1)}, u32[]{:S(2)}, u32[]{:S(2)}) collective-permute-start(f32[5,2,64,128]{3,2,1,0:T(8,128)S(1)} %shard_map.110.refs_0_.order), channel_id=1, source_target_pairs={{0,16},{8,24},{16,0},{24,8},{1,17},{9,25},{17,1},{25,9},{2,18},{10... | collective-permute-start | bytes 983048 | tf_op jit(solution)/shard_map/ppermute | solution.py:444
  9.2 1.3 %collective-permute-start = (f32[5,2,64,128]{3,2,1,0:T(8,128)S(1)}, f32[5,2,64,128]{3,2,1,0:T(8,128)S(1)}, u32[]{:S(2)}, u32[]{:S(2)}) collective-permute-start(f32[5,2,64,128]{3,2,1,0:T(8,128)S(1)} %shard_map.110.refs_0_.order), channel_id=1, source_target_pairs={{0,8},{8,0},{16,24},{24,16},{1,9},{9,1},{17,25},{25,17},{2,10},{10... | collective-permute-start | bytes 983048 | tf_op jit(solution)/shard_map/ppermute | solution.py:444
  11.1 0.7 %shard_map.111 = (f32[2,256,128]{2,1,0:T(8,128)S(1)}, f32[2,256,128]{2,1,0:T(8,128)S(1)}) custom-call(s32[1,256]{1,0:T(1,128)S(1)} %copy-done.9, f32[2,256]{1,0:T(2,128)S(1)} %bitcast.38), custom_call_target="tpu_custom_call" | custom-call | flops 1500000000 | bytes 527360 | tf_op jit(solution)/shard_map/pallas_call | solution.py:408
  11.8 1.3 %collective-permute-done.2.refs_1_ = f32[5,2,64,128]{3,2,1,0:T(8,128)S(1)} collective-permute-done((f32[5,2,64,128]{3,2,1,0:T(8,128)S(1)}, f32[5,2,64,128]{3,2,1,0:T(8,128)S(1)}, u32[]{:S(2)}, u32[]{:S(2)}) %collective-permute-start.2) | collective-permute-done | bytes 327712 | tf_op jit(solution)/shard_map/ppermute | solution.py:444
  13.7 0.9 %shard_map.114 = (f32[2,2,256,128]{3,2,1,0:T(8,128)S(1)}, f32[6,2,256,128]{3,2,1,0:T(8,128)S(1)}, f32[2,128,128]{2,1,0:T(8,128)S(1)}, f32[2,128,128]{2,1,0:T(8,128)S(1)}, f32[2,4,272,128]{3,2,1,0:T(8,128)S(1)}) custom-call(s32[2,256,128]{2,1,0:T(8,128)S(1)} %shard_map.109.order.cells, s32[1,1]{1,0:T(1,128)} %bitcast.4.source, f32[1,2]{1,0:T(1,128)S(1)} %copy-done.2, ...), custom_call_target="tpu_custom_call" | custom-call | flops 1200000000 | bytes 7667724 | tf_op jit(solution)/shard_map/pallas_call | solution.py:408
  14.6 0.7 %collective-permute-start.5 = (f32[2,128,128]{2,1,0:T(8,128)S(1)}, f32[2,128,128]{2,1,0:T(8,128)S(1)}, u32[]{:S(2)}, u32[]{:S(2)}) collective-permute-start(f32[2,128,128]{2,1,0:T(8,128)S(1)} %get-tuple-element.28), channel_id=1, source_target_pairs={{1,2},{3,4},{5,6},{2,1},{4,3},{6,5},{9,10},{11,12},{13,14},{10,9},... | collective-permute-start | bytes 393224 | tf_op jit(solution)/shard_map/ppermute | solution.py:448
  15.3 4.8 %collective-permute-start.6 = (f32[2,128,128]{2,1,0:T(8,128)S(1)}, f32[2,128,128]{2,1,0:T(8,128)S(1)}, u32[]{:S(2)}, u32[]{:S(2)}) collective-permute-start(f32[2,128,128]{2,1,0:T(8,128)S(1)} %get-tuple-element.29), channel_id=1, source_target_pairs={{0,1},{2,3},{4,5},{6,7},{1,0},{3,2},{5,4},{7,6},{8,9},{10,11},{12,... | collective-permute-start | bytes 393224 | tf_op jit(solution)/shard_map/ppermute | solution.py:448
  20.1 1.0 %shard_map.115 = (f32[7,2,256,128]{3,2,1,0:T(8,128)S(1)}, f32[2,2,256,128]{3,2,1,0:T(8,128)S(1)}, f32[6,2,256,128]{3,2,1,0:T(8,128)S(1)}, f32[2,128,128]{2,1,0:T(8,128)S(1)}, f32[2,128,128]{2,1,0:T(8,128)S(1)}) custom-call(s32[2,256,128]{2,1,0:T(8,128)S(1)} %shard_map.109.order.cells, ...), custom_call_target="tpu_custom_call", output_to_operand_aliasing={{0}: (7, {}), {1}: (8, {}), {2}: (9, {})} | custom-call | flops 1200000000 | bytes 11206668 | tf_op jit(solution)/shard_map/pallas_call | solution.py:408
  21.1 0.7 %collective-permute-start.7 = (f32[2,128,128]{2,1,0:T(8,128)S(1)}, f32[2,128,128]{2,1,0:T(8,128)S(1)}, u32[]{:S(2)}, u32[]{:S(2)}) collective-permute-start(f32[2,128,128]{2,1,0:T(8,128)S(1)} %get-tuple-element.30), channel_id=1, source_target_pairs={{1,2},{3,4},{5,6},{2,1},{4,3},{6,5},{9,10},{11,12},{13,14},{10,9},... | collective-permute-start | bytes 393224 | tf_op jit(solution)/shard_map/ppermute | solution.py:448
  21.7 3.0 %collective-permute-start.8 = (f32[2,128,128]{2,1,0:T(8,128)S(1)}, f32[2,128,128]{2,1,0:T(8,128)S(1)}, u32[]{:S(2)}, u32[]{:S(2)}) collective-permute-start(f32[2,128,128]{2,1,0:T(8,128)S(1)} %get-tuple-element.31), channel_id=1, source_target_pairs={{0,1},{2,3},{4,5},{6,7},{1,0},{3,2},{5,4},{7,6},{8,9},{10,11},{12,... | collective-permute-start | bytes 393224 | tf_op jit(solution)/shard_map/ppermute | solution.py:448
  25.5 1.4 %collective-permute-start.11 = (f32[5,2,40,128]{3,2,1,0:T(8,128)S(1)}, f32[5,2,40,128]{3,2,1,0:T(8,128)S(1)}, u32[]{:S(2)}, u32[]{:S(2)}) collective-permute-start(f32[5,2,40,128]{3,2,1,0:T(8,128)S(1)} %shard_map.118.refs_0_.order), channel_id=1, source_target_pairs={{0,8},{8,0},{16,24},{24,16},{1,9},{9,1},{17,25},{25,17},{2,10},{10... | collective-permute-start | bytes 614408 | tf_op jit(solution)/shard_map/ppermute | solution.py:444
  27.9 1.6 %collective-permute-start.13 = (f32[5,2,24,128]{3,2,1,0:T(8,128)S(1)}, f32[5,2,24,128]{3,2,1,0:T(8,128)S(1)}, u32[]{:S(2)}, u32[]{:S(2)}) collective-permute-start(f32[5,2,24,128]{3,2,1,0:T(8,128)S(1)} %shard_map.119.refs_0_), channel_id=1, source_target_pairs={{0,16},{8,24},{16,0},{24,8},{1,17},{9,25},{17,1},{25,9},{2,18},{10... | collective-permute-start | bytes 368648 | tf_op jit(solution)/shard_map/ppermute | solution.py:444
  29.7 0.6 %collective-permute-start.9 = (f32[5,2,24,128]{3,2,1,0:T(8,128)S(1)}, f32[5,2,24,128]{3,2,1,0:T(8,128)S(1)}, u32[]{:S(2)}, u32[]{:S(2)}) collective-permute-start(f32[5,2,24,128]{3,2,1,0:T(8,128)S(1)} %shard_map.121.refs_0_), channel_id=1, source_target_pairs={{0,16},{8,24},{16,0},{24,8},{1,17},{9,25},{17,1},{25,9},{2,18},{10... | collective-permute-start | bytes 368648 | tf_op jit(solution)/shard_map/ppermute | solution.py:444
  30.6 0.8 %collective-permute-start.10 = (f32[5,2,40,128]{3,2,1,0:T(8,128)S(1)}, f32[5,2,40,128]{3,2,1,0:T(8,128)S(1)}, u32[]{:S(2)}, u32[]{:S(2)}) collective-permute-start(f32[5,2,40,128]{3,2,1,0:T(8,128)S(1)} %shard_map.124.refs_0_), channel_id=1, source_target_pairs={{0,8},{8,0},{16,24},{24,16},{1,9},{9,1},{17,25},{25,17},{2,10},{10... | collective-permute-start | bytes 614408 | tf_op jit(solution)/shard_map/ppermute | solution.py:444
  32.6 1.4 %collective-permute-start.12 = (f32[5,2,40,128]{3,2,1,0:T(8,128)S(1)}, f32[5,2,40,128]{3,2,1,0:T(8,128)S(1)}, u32[]{:S(2)}, u32[]{:S(2)}) collective-permute-start(f32[5,2,40,128]{3,2,1,0:T(8,128)S(1)} %shard_map.127.order), channel_id=1, source_target_pairs={{0,16},{8,24},{16,0},{24,8},{1,17},{9,25},{17,1},{25,9},{2,18},{10... | collective-permute-start | bytes 614408 | tf_op jit(solution)/shard_map/ppermute | solution.py:444
  34.1 1.5 %collective-permute-start.14 = (f32[5,2,24,128]{3,2,1,0:T(8,128)S(1)}, f32[5,2,24,128]{3,2,1,0:T(8,128)S(1)}, u32[]{:S(2)}, u32[]{:S(2)}) collective-permute-start(f32[5,2,24,128]{3,2,1,0:T(8,128)S(1)} %shard_map.129), channel_id=1, source_target_pairs={{0,8},{8,0},{16,24},{24,16},{1,9},{9,1},{17,25},{25,17},{2,10},{10... | collective-permute-start | bytes 368648 | tf_op jit(solution)/shard_map/ppermute | solution.py:444
  35.6 0.9 %collective-permute-done.9.refs_7_ = f32[5,2,24,128]{3,2,1,0:T(8,128)S(1)} collective-permute-done((f32[5,2,24,128]{3,2,1,0:T(8,128)S(1)}, f32[5,2,24,128]{3,2,1,0:T(8,128)S(1)}, u32[]{:S(2)}, u32[]{:S(2)}) %collective-permute-start.9) | collective-permute-done | bytes 122912 | tf_op jit(solution)/shard_map/ppermute | solution.py:444
  36.7 1.2 %collective-permute-done.10.refs_6_ = f32[5,2,40,128]{3,2,1,0:T(8,128)S(1)} collective-permute-done((f32[5,2,40,128]{3,2,1,0:T(8,128)S(1)}, f32[5,2,40,128]{3,2,1,0:T(8,128)S(1)}, u32[]{:S(2)}, u32[]{:S(2)}) %collective-permute-start.10) | collective-permute-done | bytes 204832 | tf_op jit(solution)/shard_map/ppermute | solution.py:444
  38.3 1.3 %collective-permute-done.14.refs_3_ = f32[5,2,24,128]{3,2,1,0:T(8,128)S(1)} collective-permute-done((f32[5,2,24,128]{3,2,1,0:T(8,128)S(1)}, f32[5,2,24,128]{3,2,1,0:T(8,128)S(1)}, u32[]{:S(2)}, u32[]{:S(2)}) %collective-permute-start.14) | collective-permute-done | bytes 122912 | tf_op jit(solution)/shard_map/ppermute | solution.py:444
  40.0 0.8 %shard_map.130 = f32[5,2,64,128]{3,2,1,0:T(8,128)} custom-call(f32[5,2,40,128]{3,2,1,0:T(8,128)S(1)} %shard_map.125.refs_0_, f32[5,2,40,128]{3,2,1,0:T(8,128)S(1)} %collective-permute-done.12.refs_1_, f32[5,2,24,128]{3,2,1,0:T(8,128)S(1)} %shard_map.122.refs_0_.refs_2_, f32[5,2,24,128]{3,2,1,0:T(8,128)S(1)} %collective-permute-done.14.refs_3_), custom_call_target="tpu_custom_call" | custom-call | flops 800000000 | bytes 983040 | tf_op jit(solution)/shard_map/pallas_call | solution.py:408
  (48 shorter events, 5.6 us)
Async XLA Ops:
  0.0 0.8 %copy-start.7 = (f32[2,64,128]{2,1,0:T(8,128)S(1)}, f32[2,64,128]{2,1,0:T(8,128)}, u32[]{:S(2)}) copy-start(f32[2,64,128]{2,1,0:T(8,128)} %refs_4_.1) | copy-start | bytes 196612
  0.0 0.9 %copy-start.6 = (f32[2,64,128]{2,1,0:T(8,128)S(1)}, f32[2,64,128]{2,1,0:T(8,128)}, u32[]{:S(2)}) copy-start(f32[2,64,128]{2,1,0:T(8,128)} %refs_3_.1) | copy-start | bytes 196612
  0.0 0.9 %copy-start.5 = (f32[2,64,128]{2,1,0:T(8,128)S(1)}, f32[2,64,128]{2,1,0:T(8,128)}, u32[]{:S(2)}) copy-start(f32[2,64,128]{2,1,0:T(8,128)} %refs_2_.1) | copy-start | bytes 196612
  0.0 0.9 %copy-start.4 = (f32[2,64,128]{2,1,0:T(8,128)S(1)}, f32[2,64,128]{2,1,0:T(8,128)}, u32[]{:S(2)}) copy-start(f32[2,64,128]{2,1,0:T(8,128)} %refs_1_.1) | copy-start | bytes 196612
  0.0 1.0 %copy-start.3 = (f32[2,64,128]{2,1,0:T(8,128)S(1)}, f32[2,64,128]{2,1,0:T(8,128)}, u32[]{:S(2)}) copy-start(f32[2,64,128]{2,1,0:T(8,128)} %refs_0_.1) | copy-start | bytes 196612
  0.0 4.9 %copy-start.1 = (f32[1,4,2,256,128]{4,3,2,1,0:T(8,128)S(1)}, f32[1,4,2,256,128]{4,3,2,1,0:T(8,128)}, u32[]{:S(2)}) copy-start(f32[1,4,2,256,128]{4,3,2,1,0:T(8,128)} %param.16) | copy-start | bytes 3145732
  1.0 4.0 %copy-start = (f32[1,4,2,256,128]{4,3,2,1,0:T(8,128)S(1)}, f32[1,4,2,256,128]{4,3,2,1,0:T(8,128)}, u32[]{:S(2)}) copy-start(f32[1,4,2,256,128]{4,3,2,1,0:T(8,128)} %param.17) | copy-start | bytes 3145732
  1.0 10.2 %copy-start.8 = (f32[1,2,256]{2,1,0:T(2,128)S(1)}, f32[1,2,256]{2,1,0:T(2,128)}, u32[]{:S(2)}) copy-start(f32[1,2,256]{2,1,0:T(2,128)} %param.21) | copy-start | bytes 6148
  1.0 10.2 %copy-start.9 = (s32[1,256]{1,0:T(1,128)S(1)}, s32[1,256]{1,0:T(1,128)}, u32[]{:S(2)}) copy-start(s32[1,256]{1,0:T(1,128)} %receivers.1) | copy-start | bytes 3076
  1.0 12.1 %collective-permute-start.2 = (f32[5,2,64,128]{3,2,1,0:T(8,128)S(1)}, f32[5,2,64,128]{3,2,1,0:T(8,128)S(1)}, u32[]{:S(2)}, u32[]{:S(2)}) collective-permute-start(f32[5,2,64,128]{3,2,1,0:T(8,128)S(1)} %shard_map.110.refs_0_.order), channel_id=1, source_target_pairs={{0,24},{8,16},{16,8},{24,0},{1,25},{9,17},{17,9},{25,1},{2,26},{10... | collective-permute-start | bytes 983048 | tf_op jit(solution)/shard_map/ppermute | solution.py:444
  5.0 8.3 %collective-permute-start.3 = (f32[4,256,128]{2,1,0:T(8,128)S(1)}, f32[4,256,128]{2,1,0:T(8,128)S(1)}, u32[]{:S(2)}, u32[]{:S(2)}) collective-permute-start(f32[4,256,128]{2,1,0:T(8,128)S(1)} %get-tuple-element.22), channel_id=1, source_target_pairs={{1,2},{3,4},{5,6},{2,1},{4,3},{6,5},{9,10},{11,12},{13,14},{10,9},... | collective-permute-start | bytes 1572872 | tf_op jit(solution)/shard_map/ppermute | solution.py:448
  5.7 7.7 %collective-permute-start.4 = (f32[4,256,128]{2,1,0:T(8,128)S(1)}, f32[4,256,128]{2,1,0:T(8,128)S(1)}, u32[]{:S(2)}, u32[]{:S(2)}) collective-permute-start(f32[4,256,128]{2,1,0:T(8,128)S(1)} %get-tuple-element.23), channel_id=1, source_target_pairs={{0,1},{2,3},{4,5},{6,7},{1,0},{3,2},{5,4},{7,6},{8,9},{10,11},{12,... | collective-permute-start | bytes 1572872 | tf_op jit(solution)/shard_map/ppermute | solution.py:448
  8.7 11.4 %collective-permute-start.1 = (f32[5,2,64,128]{3,2,1,0:T(8,128)S(1)}, f32[5,2,64,128]{3,2,1,0:T(8,128)S(1)}, u32[]{:S(2)}, u32[]{:S(2)}) collective-permute-start(f32[5,2,64,128]{3,2,1,0:T(8,128)S(1)} %shard_map.110.refs_0_.order), channel_id=1, source_target_pairs={{0,16},{8,24},{16,0},{24,8},{1,17},{9,25},{17,1},{25,9},{2,18},{10... | collective-permute-start | bytes 983048 | tf_op jit(solution)/shard_map/ppermute | solution.py:444
  9.2 10.9 %collective-permute-start = (f32[5,2,64,128]{3,2,1,0:T(8,128)S(1)}, f32[5,2,64,128]{3,2,1,0:T(8,128)S(1)}, u32[]{:S(2)}, u32[]{:S(2)}) collective-permute-start(f32[5,2,64,128]{3,2,1,0:T(8,128)S(1)} %shard_map.110.refs_0_.order), channel_id=1, source_target_pairs={{0,8},{8,0},{16,24},{24,16},{1,9},{9,1},{17,25},{25,17},{2,10},{10... | collective-permute-start | bytes 983048 | tf_op jit(solution)/shard_map/ppermute | solution.py:444
  14.6 10.1 %collective-permute-start.5 = (f32[2,128,128]{2,1,0:T(8,128)S(1)}, f32[2,128,128]{2,1,0:T(8,128)S(1)}, u32[]{:S(2)}, u32[]{:S(2)}) collective-permute-start(f32[2,128,128]{2,1,0:T(8,128)S(1)} %get-tuple-element.28), channel_id=1, source_target_pairs={{1,2},{3,4},{5,6},{2,1},{4,3},{6,5},{9,10},{11,12},{13,14},{10,9},... | collective-permute-start | bytes 393224 | tf_op jit(solution)/shard_map/ppermute | solution.py:448
  15.3 9.5 %collective-permute-start.6 = (f32[2,128,128]{2,1,0:T(8,128)S(1)}, f32[2,128,128]{2,1,0:T(8,128)S(1)}, u32[]{:S(2)}, u32[]{:S(2)}) collective-permute-start(f32[2,128,128]{2,1,0:T(8,128)S(1)} %get-tuple-element.29), channel_id=1, source_target_pairs={{0,1},{2,3},{4,5},{6,7},{1,0},{3,2},{5,4},{7,6},{8,9},{10,11},{12,... | collective-permute-start | bytes 393224 | tf_op jit(solution)/shard_map/ppermute | solution.py:448
  21.1 6.5 %collective-permute-start.7 = (f32[2,128,128]{2,1,0:T(8,128)S(1)}, f32[2,128,128]{2,1,0:T(8,128)S(1)}, u32[]{:S(2)}, u32[]{:S(2)}) collective-permute-start(f32[2,128,128]{2,1,0:T(8,128)S(1)} %get-tuple-element.30), channel_id=1, source_target_pairs={{1,2},{3,4},{5,6},{2,1},{4,3},{6,5},{9,10},{11,12},{13,14},{10,9},... | collective-permute-start | bytes 393224 | tf_op jit(solution)/shard_map/ppermute | solution.py:448
  21.7 5.8 %collective-permute-start.8 = (f32[2,128,128]{2,1,0:T(8,128)S(1)}, f32[2,128,128]{2,1,0:T(8,128)S(1)}, u32[]{:S(2)}, u32[]{:S(2)}) collective-permute-start(f32[2,128,128]{2,1,0:T(8,128)S(1)} %get-tuple-element.31), channel_id=1, source_target_pairs={{0,1},{2,3},{4,5},{6,7},{1,0},{3,2},{5,4},{7,6},{8,9},{10,11},{12,... | collective-permute-start | bytes 393224 | tf_op jit(solution)/shard_map/ppermute | solution.py:448
  25.5 7.1 %collective-permute-start.11 = (f32[5,2,40,128]{3,2,1,0:T(8,128)S(1)}, f32[5,2,40,128]{3,2,1,0:T(8,128)S(1)}, u32[]{:S(2)}, u32[]{:S(2)}) collective-permute-start(f32[5,2,40,128]{3,2,1,0:T(8,128)S(1)} %shard_map.118.refs_0_.order), channel_id=1, source_target_pairs={{0,8},{8,0},{16,24},{24,16},{1,9},{9,1},{17,25},{25,17},{2,10},{10... | collective-permute-start | bytes 614408 | tf_op jit(solution)/shard_map/ppermute | solution.py:444
  27.9 6.2 %collective-permute-start.13 = (f32[5,2,24,128]{3,2,1,0:T(8,128)S(1)}, f32[5,2,24,128]{3,2,1,0:T(8,128)S(1)}, u32[]{:S(2)}, u32[]{:S(2)}) collective-permute-start(f32[5,2,24,128]{3,2,1,0:T(8,128)S(1)} %shard_map.119.refs_0_), channel_id=1, source_target_pairs={{0,16},{8,24},{16,0},{24,8},{1,17},{9,25},{17,1},{25,9},{2,18},{10... | collective-permute-start | bytes 368648 | tf_op jit(solution)/shard_map/ppermute | solution.py:444
  29.7 6.8 %collective-permute-start.9 = (f32[5,2,24,128]{3,2,1,0:T(8,128)S(1)}, f32[5,2,24,128]{3,2,1,0:T(8,128)S(1)}, u32[]{:S(2)}, u32[]{:S(2)}) collective-permute-start(f32[5,2,24,128]{3,2,1,0:T(8,128)S(1)} %shard_map.121.refs_0_), channel_id=1, source_target_pairs={{0,16},{8,24},{16,0},{24,8},{1,17},{9,25},{17,1},{25,9},{2,18},{10... | collective-permute-start | bytes 368648 | tf_op jit(solution)/shard_map/ppermute | solution.py:444
  30.6 7.3 %collective-permute-start.10 = (f32[5,2,40,128]{3,2,1,0:T(8,128)S(1)}, f32[5,2,40,128]{3,2,1,0:T(8,128)S(1)}, u32[]{:S(2)}, u32[]{:S(2)}) collective-permute-start(f32[5,2,40,128]{3,2,1,0:T(8,128)S(1)} %shard_map.124.refs_0_), channel_id=1, source_target_pairs={{0,8},{8,0},{16,24},{24,16},{1,9},{9,1},{17,25},{25,17},{2,10},{10... | collective-permute-start | bytes 614408 | tf_op jit(solution)/shard_map/ppermute | solution.py:444
  32.6 7.3 %collective-permute-start.12 = (f32[5,2,40,128]{3,2,1,0:T(8,128)S(1)}, f32[5,2,40,128]{3,2,1,0:T(8,128)S(1)}, u32[]{:S(2)}, u32[]{:S(2)}) collective-permute-start(f32[5,2,40,128]{3,2,1,0:T(8,128)S(1)} %shard_map.127.order), channel_id=1, source_target_pairs={{0,16},{8,24},{16,0},{24,8},{1,17},{9,25},{17,1},{25,9},{2,18},{10... | collective-permute-start | bytes 614408 | tf_op jit(solution)/shard_map/ppermute | solution.py:444
  34.1 5.5 %collective-permute-start.14 = (f32[5,2,24,128]{3,2,1,0:T(8,128)S(1)}, f32[5,2,24,128]{3,2,1,0:T(8,128)S(1)}, u32[]{:S(2)}, u32[]{:S(2)}) collective-permute-start(f32[5,2,24,128]{3,2,1,0:T(8,128)S(1)} %shard_map.129), channel_id=1, source_target_pairs={{0,8},{8,0},{16,24},{24,16},{1,9},{9,1},{17,25},{25,17},{2,10},{10... | collective-permute-start | bytes 368648 | tf_op jit(solution)/shard_map/ppermute | solution.py:444
  (1 other events, 0.7 us)
